TPU v7x, 512 devices: a whole 4x8x8 slice. The times are simulated.
512 devices in a mesh: grp: 8 (over z_hi, core), seq: 8 (over z_lo, x), tp: 8 (over y).
Axes of the slice: x: 4, y: 8, z: 8 (z_hi: 4, z_lo: 2; z = z_hi * 2 + z_lo), core: 2. Of those that a mesh axis runs over, the one named last changes fastest.
Arguments:
- queries: bfloat16 [4, 2048, 8192], P(None, ('grp', 'seq'), 'tp'), may hold values from -6 to 6
- new_token_cache: bfloat16 [4, 2048, 2048], P(None, ('grp', 'seq'), 'tp'), may hold values from -6 to 6
- kv_pool: bfloat16 [4096, 16, 2048], P(('grp', 'seq'), None, 'tp'), may hold values from -6 to 6
- block_table: int32 [2048, 2], P(('grp', 'seq')), may hold values from 0 to 63, as said below
- context_len: int32 [64, 32], P(('grp', 'seq')), may hold values from 1 to 32, 512 in all within a row
- out_proj: bfloat16 [8192, 8192], P('tp', 'seq'), may hold values from -0.09375 to 0.09375
- finished_prompt_cache: bfloat16 [4096, 16, 2048], P(('grp', 'seq'), None, 'tp'), may hold values from -6 to 6
- prompt_blocks: int32 [64, 32], P(('grp', 'seq')), may hold values from 1 to 3, as said below
- prompt_tail: int32 [64, 32], P(('grp', 'seq')), may hold values from 1 to 16
- prompt_owner: int32 [64, 32], P(('grp', 'seq')), may hold values from 0 to 63, as said below
Outputs:
- decoded: bfloat16 [4, 2048, 8192], P(None, 'grp', ('seq', 'tp'))
- migrated: bfloat16 [12288, 16, 2048], P(('grp', 'seq'), None, 'tp')
Inputs may be any that keep to these rules, and one draw needn't show every extreme that they name: `block_table`: within the 32 rows of each device the entries are a permutation of the device's local page numbers 0 to 63. `context_len`: the 32 lengths of one device sum to half of 1024. `prompt_blocks`: the 32 entries of one device sum to 64; the first prompt of every device has 3 blocks. `prompt_owner`: the 32 owners of one device are distinct; the first prompts of all devices have one common owner.
All inputs are finite; a program needn't handle non-finite values.
Results may differ from a plain program's by a relative error of at most 0.015.
Values may be sent and summed in bfloat16 or wider, within the bound.
No kernel may reach another device: no remote copies, remote signals or barrier semaphores. Data moves between devices by JAX's collectives and lax.ppermute only.
A program may use at most 64 MiB of HBM per device.

v0:
```python
import jax
import jax.numpy as jnp
from jax import lax
from jax.sharding import PartitionSpec as P

QUERY_HEADS = 64
KEY_VALUE_HEADS = 8
HEAD_SIZE = 128
PAGE_TOKENS = 16
CAP = 3


NEGATIVE = -1e30


def attend(query_block, fresh_block, pool_block, table_block, length_row):
    steps = query_block.shape[0]
    rows = query_block.shape[1]
    kv_heads = pool_block.shape[2] // (2 * HEAD_SIZE)
    head_groups = QUERY_HEADS // KEY_VALUE_HEADS
    context = table_block.shape[1] * pool_block.shape[1]
    gathered = pool_block[table_block].reshape(rows, context, kv_heads, 2, HEAD_SIZE)
    key_rows = gathered[:, :, :, 0, :]
    value_rows = gathered[:, :, :, 1, :]
    fresh = fresh_block.reshape(steps, rows, kv_heads, 2, HEAD_SIZE)
    fresh_keys = fresh[:, :, :, 0, :]
    fresh_values = fresh[:, :, :, 1, :]
    query_heads = query_block.reshape(steps, rows, kv_heads, head_groups, HEAD_SIZE)
    scale = HEAD_SIZE ** (-0.5)
    cached = (
        jnp.einsum("srhgd,rchd->srhgc", query_heads, key_rows, preferred_element_type=jnp.float32)
        * scale
    )
    recent = (
        jnp.einsum("srhgd,urhd->srhgu", query_heads, fresh_keys, preferred_element_type=jnp.float32)
        * scale
    )
    live_cached = jnp.arange(context)[None, :] < length_row[:, None]
    live_cached = jnp.broadcast_to(live_cached[None, :, None, None, :], cached.shape)
    live_recent = jnp.arange(steps)[None, :] <= jnp.arange(steps)[:, None]
    live_recent = jnp.broadcast_to(live_recent[:, None, None, None, :], recent.shape)
    scores = jnp.concatenate([cached, recent], -1)
    live = jnp.concatenate([live_cached, live_recent], -1)
    masked_scores = jnp.where(live, scores, NEGATIVE)
    row_max = jnp.max(masked_scores, -1, keepdims=True)
    raw = jnp.where(live, jnp.exp(masked_scores - row_max), 0.0)
    probs = (raw / jnp.sum(raw, -1, keepdims=True)).astype(jnp.bfloat16)
    mixed = jnp.einsum(
        "srhgc,rchd->srhgd", probs[..., :context], value_rows, preferred_element_type=jnp.float32
    )
    mixed = mixed + jnp.einsum(
        "srhgu,urhd->srhgd", probs[..., context:], fresh_values, preferred_element_type=jnp.float32
    )
    return mixed.astype(jnp.bfloat16).reshape(steps, rows, kv_heads * head_groups * HEAD_SIZE)


def pack_blocks(finished_prompt_cache, prompt_blocks, prompt_tail, prompt_owner):
    count = finished_prompt_cache.shape[0]
    runs = prompt_blocks[0]
    ends = jnp.cumsum(runs)
    starts = ends - runs
    local = jnp.arange(count, dtype=jnp.int32)
    inside = (local[:, None] >= starts[None, :]) & (local[:, None] < ends[None, :])

    def pick(table):
        return jnp.sum(jnp.where(inside, table[None, :], 0), 1)

    owner = pick(prompt_owner[0])
    slot = local - pick(starts)
    last = local == pick(ends) - 1
    valid = jnp.where(last, pick(prompt_tail[0]), PAGE_TOKENS)
    receivers = lax.axis_size("grp") * lax.axis_size("seq") * CAP
    target_slot = owner * CAP + slot
    selector = (jnp.arange(receivers)[:, None] == target_slot[None, :]).astype(jnp.bfloat16)
    keep = jnp.arange(PAGE_TOKENS)[None, :, None] < valid[:, None, None]
    masked_scores = jnp.where(keep, finished_prompt_cache, jnp.zeros_like(finished_prompt_cache))
    packed = jnp.dot(
        selector, masked_scores.reshape(count, -1), preferred_element_type=jnp.float32
    ).astype(jnp.bfloat16)
    return packed.reshape(receivers, PAGE_TOKENS, finished_prompt_cache.shape[2])


def per_device(
    queries,
    new_token_cache,
    kv_pool,
    block_table,
    context_len,
    out_proj,
    finished_prompt_cache,
    prompt_blocks,
    prompt_tail,
    prompt_owner,
):
    heads = attend(queries, new_token_cache, kv_pool, block_table, context_len[0])
    partial_sums = jnp.einsum(
        "srk,kc->src",
        lax.all_gather(heads, "seq", axis=1, tiled=True),
        out_proj,
        preferred_element_type=jnp.float32,
    )
    decoded = lax.psum_scatter(partial_sums, "tp", scatter_dimension=2, tiled=True).astype(
        jnp.bfloat16
    )
    packed = pack_blocks(finished_prompt_cache, prompt_blocks, prompt_tail, prompt_owner)
    migrated = lax.all_to_all(packed, ("grp", "seq"), split_axis=0, concat_axis=0, tiled=True)
    return (decoded, migrated)


def solution(mesh):
    placed = (
        P(None, ("grp", "seq"), "tp"),
        P(None, ("grp", "seq"), "tp"),
        P(("grp", "seq"), None, "tp"),
        P(("grp", "seq"), None),
        P(("grp", "seq"), None),
        P("tp", "seq"),
        P(("grp", "seq"), None, "tp"),
        P(("grp", "seq"), None),
        P(("grp", "seq"), None),
        P(("grp", "seq"), None),
    )
    return jax.shard_map(
        per_device,
        mesh=mesh,
        in_specs=placed,
        out_specs=(P(None, "grp", ("seq", "tp")), P(("grp", "seq"), None, "tp")),
        check_vma=False,
    )
```

profile of v0, /device:TPU:1, one launch (start us, length us, event | category | flops | bytes accessed | tf_op | source)
XLA Modules:
  0.0 144.0 jit_solution(3684219978976281338)
XLA Ops:
  7.2 0.0 copy-start
  7.2 0.0 all-gather.2.cloned.1.call-start
  7.2 0.8 compare_select_fusion
  8.1 0.1 copy.30
  8.1 0.1 reshape.311
  8.3 0.0 copy-start.2
  8.3 1.7 %gather_fusion = bf16[64,16,256]{2,1,0:T(8,128)(2,1)S(1)} fusion(bf16[64,16,256]{2,1,0:T(8,128)(2,1)} %param.12, s32[1024]{0:T(1024)S(1)} %pad_clamp_fusion), kind=kCustom, calls=%fused_computation | custom fusion | bytes 1048832 | tf_op jit(solution)/shard_map/gather | solution.py:22
  10.0 0.0 copy-start.3
  10.0 0.0 copy-start.4
  10.0 0.1 reshape.295
  10.1 2.0 %fusion.15 = (bf16[32,32,1,1,128]{4,3,1,0,2:T(2,128)(2,1)S(1)}, bf16[32,32,1,1,128]{4,3,1,0,2:T(2,128)(2,1)}) fusion(bf16[32,32,1,2,128]{4,3,1,0,2:T(2,128)(2,1)S(1)} %reshape.295), kind=kLoop, calls=%fused_computation.46 | loop fusion | bytes 1048576 | tf_op jit(solution)/shard_map/slice | solution.py:24
  12.1 0.0 copy-done.2
  12.2 0.0 copy-done.3
  12.2 0.1 fusion.16
  12.3 0.0 copy-done.4
  12.3 0.1 iota_compare_fusion.5
  12.4 1.3 fusion.4
  13.7 0.2 fusion.3
  14.0 0.6 fusion.14
  14.5 0.7 fusion.7
  15.2 0.6 divide_convert_fusion
  15.9 0.2 fusion.8
  16.1 0.3 fusion.6
  16.4 0.1 reshape.304
  16.4 0.8 copy.39
  17.2 0.0 all-gather.2.cloned.1.call-update
  17.2 0.0 reduce-scatter.2.cloned.1.call-start
  17.3 47.8 %all-gather.2.cloned.1.call-done = bf16[4,256,1024]{2,1,0:T(8,128)(2,1)} async-done(((bf16[4,32,1024]{2,1,0:T(8,128)(2,1)}), bf16[4,256,1024]{2,1,0:T(8,128)(2,1)}) %all-gather.2.cloned.1.call-update) | async-done | bytes 2097168 | tf_op jit(solution)/shard_map/all_gather | solution.py:98
  65.1 0.0 copy-done
  65.1 5.8 %fusion = f32[4,256,1024]{2,1,0:T(8,128)} fusion(bf16[4,256,1024]{2,1,0:T(8,128)(2,1)} %all-gather.2.cloned.1.call-done, bf16[1024,1024]{1,0:T(8,128)(2,1)S(1)} %copy-done), kind=kOutput, calls=%fused_computation.2 | convolution fusion | flops 2147483648 | bytes 8388608 | tf_op jit(solution)/shard_map/srk,kc->src/dot_general | solution.py:96
  70.9 0.0 reduce-scatter.2.cloned.1.call-update
  70.9 0.6 copy-done.5
  71.6 0.1 copy.40
  71.7 0.1 reduce-window.4
  71.7 0.1 reduce.2
  71.8 0.0 copy-done.6
  71.8 0.0 copy-done.7
  71.9 0.1 select_reduce_fusion.3
  72.0 0.1 iota_compare_fusion.2
  72.0 0.0 copy-done.1
  72.1 0.2 broadcast_select_fusion
  72.3 0.2 copy.52
  72.4 0.6 convolution_convert_fusion
  73.0 0.4 copy.53
  73.4 52.7 %all_to_all.5 = bf16[192,16,256]{2,1,0:T(8,128)(2,1)} all-to-all(bf16[192,16,256]{2,1,0:T(8,128)(2,1)S(1)} %bitcast.94), channel_id=1, replica_groups=mesh['grp'=8,'seq'=8,'tp'=8] {'grp','seq'}, dimensions={0} | all-to-all | bytes 3145728 | tf_op jit(solution)/shard_map/all_to_all | solution.py:106
  126.1 6.7 %reduce-scatter.2.cloned.1.call-done = f32[4,256,128]{2,1,0:T(8,128)} async-done(((f32[4,256,1024]{2,1,0:T(8,128)}), f32[4,256,128]{2,1,0:T(8,128)}) %reduce-scatter.2.cloned.1.call-update) | async-done | bytes 524304 | tf_op jit(solution)/shard_map/reduce_scatter | solution.py:102
  132.8 1.8 %convert_element_type.31 = bf16[4,256,128]{2,1,0:T(8,128)(2,1)} convert(f32[4,256,128]{2,1,0:T(8,128)} %reduce-scatter.2.cloned.1.call-done) | non-fusion elementwise | flops 131072 | bytes 786432 | tf_op jit(solution)/shard_map/convert_element_type | solution.py:102
  134.5 2.7 %copy.67 = bf16[192,16,256]{2,1,0:T(8,128)(2,1)} copy(bf16[192,16,256]{2,1,0:T(8,128)(2,1)} %all_to_all.5) | data formatting | bytes 3145728
  (12 shorter events, 0.2 us)
Async XLA Ops:
  7.2 57.9 %copy-start = (bf16[1024,1024]{1,0:T(8,128)(2,1)S(1)}, bf16[1024,1024]{1,0:T(8,128)(2,1)}, u32[]{:S(2)}) copy-start(bf16[1024,1024]{1,0:T(8,128)(2,1)} %param.15) | copy-start | bytes 6291460
  7.2 57.9 %all-gather.2.cloned.1.call-start = ((), (), s32[]{:S(2)}) async-start(), calls=%async_computation.2 | async-start | bytes 2359296 | tf_op jit(solution)/shard_map/all_gather | solution.py:98
  8.3 3.8 %copy-start.2 = (bf16[4,32,1024]{2,1,0:T(8,128)(2,1)S(1)}, bf16[4,32,1024]{2,1,0:T(8,128)(2,1)}, u32[]{:S(2)}) copy-start(bf16[4,32,1024]{2,1,0:T(8,128)(2,1)} %param.10) | copy-start | bytes 786436
  10.0 2.2 %copy-start.3 = (bf16[4,32,256]{2,1,0:T(8,128)(2,1)S(1)}, bf16[4,32,256]{2,1,0:T(8,128)(2,1)}, u32[]{:S(2)}) copy-start(bf16[4,32,256]{2,1,0:T(8,128)(2,1)} %param.11) | copy-start | bytes 196612
  10.0 2.3 %copy-start.4 = (s32[1,32]{1,0:T(1,128)S(1)}, s32[1,32]{1,0:T(1,128)}, u32[]{:S(2)}) copy-start(s32[1,32]{1,0:T(1,128)} %param.14) | copy-start | bytes 388
  17.2 115.5 %reduce-scatter.2.cloned.1.call-start = ((), (), s32[]{:S(2)}) async-start(), calls=%async_computation.3 | async-start | bytes 4718592 | tf_op jit(solution)/shard_map/reduce_scatter | solution.py:102
  70.9 0.7 copy-start.5
  70.9 0.9 copy-start.6
  70.9 0.9 copy-start.7
  70.9 1.1 copy-start.1
Sparse Core Ops, SparseCore 0:
  17.4 47.6 all-gather.1
  71.1 61.6 reduce-scatter.1
where the time goes:
time: 144 us
  waiting for transfers between devices  54.5 us (38%)
  blocking collectives  52.7 us (37%)
  between operations  14.3 us (10%)
  local copies, waits for them, and re-layouts  9.07 us (6%)
  matrix products  8.4 us (6%)
  other arithmetic  5.12 us (4%)
    all_to_all x1, blocking collectives, per_device(): lax.all_to_all(packed, ('grp', 'seq'), split_axis=0, concat_axis=0, tiled...  52.7 us
    all_gather x1, waiting for transfers between devices, per_device(): lax.all_gather(heads, 'seq', axis=1, tiled=True)  47.8 us
    reduce_scatter x1, waiting for transfers between devices, per_device(): lax.psum_scatter(partial_sums, 'tp', scatter_dimension=2, tiled=True)  6.66 us
    dot_general x1, matrix products, per_device(): jnp.einsum('srk,kc->src', lax.all_gather(heads, 'seq', axis=1, tiled=True...  5.85 us
    unnamed x20, local copies, waits for them, and re-layouts  3.97 us
  transfers between devices with their start and end apart: 2, of which 2 were waited for; matrix products, arithmetic and copies ran while one was open for 1% of the time, Pallas kernels for 0%

commit v1 on v0

v1 whole, which is shorter than its diff:
```python
import jax
import jax.numpy as jnp
from jax import lax
from jax.experimental import pallas as pl
from jax.experimental.pallas import tpu as pltpu
from jax.sharding import PartitionSpec as P

HEAD_SIZE = 128
PAGE_TOKENS = 16
CAP = 3
NEGATIVE = -1e30
OFFSETS = (4, 3, -3, 2, -2, 1, -1, 0)
GROUP = 16


def attend_kernel(
    table_hbm,
    length_hbm,
    queries_hbm,
    fresh_hbm,
    pool_hbm,
    out,
    table,
    length,
    queries,
    fresh,
    pool,
    key_rows,
    value_rows,
    arrived,
):
    loads = [
        pltpu.make_async_copy(source, target, arrived.at[i])
        for i, (source, target) in enumerate(
            (
                (table_hbm, table),
                (length_hbm, length),
                (pool_hbm, pool),
                (fresh_hbm, fresh),
                (queries_hbm, queries),
            )
        )
    ]
    for load in loads:
        load.start()
    steps, rows, width = queries.shape
    heads = width // HEAD_SIZE
    pages = table.shape[0]
    context = pages * PAGE_TOKENS
    cached = GROUP * context
    recent = steps * GROUP
    scale = HEAD_SIZE ** (-0.5)

    def index(columns, axis):
        return lax.broadcasted_iota(jnp.int32, (GROUP, columns), axis)

    own_cached = index(cached, 1) // context == index(cached, 0)
    cached_place = index(cached, 1) % context
    own_recent = index(recent, 1) % GROUP == index(recent, 0)
    recent_bias = [
        jnp.where(own_recent & (index(recent, 1) // GROUP <= s), 0.0, NEGATIVE)
        for s in range(steps)
    ]
    tile_row = index(cached, 0)
    for load in loads:
        load.wait()
    for first in range(0, rows, GROUP):
        limit = jnp.zeros((GROUP, cached), jnp.int32)
        for r in range(GROUP):
            limit = jnp.where(tile_row == r, length[0, first + r], limit)
            for j in range(pages):
                page = pool[table[j, first + r]]
                at = pl.ds(r * context + j * PAGE_TOKENS, PAGE_TOKENS)
                key_rows[at, :] = page[:, :HEAD_SIZE]
                value_rows[at, :] = page[:, HEAD_SIZE:]
        for u in range(steps):
            token = fresh[u, pl.ds(first, GROUP), :]
            at = pl.ds(cached + u * GROUP, GROUP)
            key_rows[at, :] = token[:, :HEAD_SIZE]
            value_rows[at, :] = token[:, HEAD_SIZE:]
        cached_bias = jnp.where(own_cached & (cached_place < limit), 0.0, NEGATIVE)
        for s in range(steps):
            query = jnp.concatenate(
                [
                    queries[s, pl.ds(first, GROUP), h * HEAD_SIZE : (h + 1) * HEAD_SIZE]
                    for h in range(heads)
                ],
                0,
            )
            scores = lax.dot_general(
                query, key_rows[...], (((1,), (1,)), ((), ())), preferred_element_type=jnp.float32
            )
            bias = jnp.concatenate([cached_bias, recent_bias[s]], 1)
            scores = scores.reshape(heads, GROUP, cached + recent) * scale + bias[None]
            raw = jnp.exp(scores - jnp.max(scores, -1, keepdims=True))
            probs = (raw * (1.0 / jnp.sum(raw, -1, keepdims=True))).astype(jnp.bfloat16)
            mixed = jnp.dot(
                probs.reshape(heads * GROUP, cached + recent),
                value_rows[...],
                preferred_element_type=jnp.float32,
            ).astype(jnp.bfloat16)
            for h in range(heads):
                piece = mixed[h * GROUP : (h + 1) * GROUP]
                for copy in range(out.shape[0]):
                    out[copy, s, pl.ds(first, GROUP), h * HEAD_SIZE : (h + 1) * HEAD_SIZE] = piece


def attend(copies, queries, fresh, pool, table, length):
    steps, rows, width = queries.shape
    table = table.T
    keys = GROUP * (table.shape[0] * PAGE_TOKENS + steps)
    far = pl.BlockSpec(memory_space=pltpu.HBM)
    return pl.pallas_call(
        attend_kernel,
        out_shape=jax.ShapeDtypeStruct((copies, steps, rows, width), jnp.bfloat16),
        in_specs=[far] * 5,
        out_specs=pl.BlockSpec(memory_space=pltpu.VMEM),
        scratch_shapes=[
            pltpu.SMEM(table.shape, jnp.int32),
            pltpu.SMEM(length.shape, jnp.int32),
            pltpu.VMEM(queries.shape, queries.dtype),
            pltpu.VMEM(fresh.shape, fresh.dtype),
            pltpu.VMEM(pool.shape, pool.dtype),
            pltpu.VMEM((keys, HEAD_SIZE), jnp.bfloat16),
            pltpu.VMEM((keys, HEAD_SIZE), jnp.bfloat16),
            pltpu.SemaphoreType.DMA((5,)),
        ],
        compiler_params=pltpu.CompilerParams(vmem_limit_bytes=24 << 20),
        cost_estimate=pl.CostEstimate(
            flops=4 * steps * rows * (width // HEAD_SIZE) * keys * HEAD_SIZE,
            bytes_accessed=4 << 20,
            transcendentals=0,
        ),
        name="attend",
    )(table, length, queries, fresh, pool)


def pack_kernel(blocks, tail, owner, finished, out):
    out[...] = jnp.zeros_like(out)
    count = finished.shape[0]
    token = lax.broadcasted_iota(jnp.int32, finished.shape[1:], 0)

    def one(j, start):
        held = blocks[0, j]
        for slot in range(CAP):
            valid = jnp.where(slot == held - 1, tail[0, j], PAGE_TOKENS)
            valid = jnp.where(slot < held, valid, 0)
            block = finished[jnp.minimum(start + slot, count - 1)]
            out[owner[0, j] * CAP + slot] = jnp.where(token < valid, block, jnp.zeros_like(block))
        return start + held

    lax.fori_loop(0, blocks.shape[1], one, jnp.int32(0))


def pack(receivers, finished, blocks, tail, owner):
    smem = pl.BlockSpec(memory_space=pltpu.SMEM)
    vmem = pl.BlockSpec(memory_space=pltpu.VMEM)
    return pl.pallas_call(
        pack_kernel,
        out_shape=jax.ShapeDtypeStruct((receivers * CAP,) + finished.shape[1:], finished.dtype),
        in_specs=[smem, smem, smem, vmem],
        out_specs=vmem,
        compiler_params=pltpu.CompilerParams(vmem_limit_bytes=16 << 20),
        cost_estimate=pl.CostEstimate(flops=0, bytes_accessed=2 << 20, transcendentals=0),
        name="pack",
    )(blocks, tail, owner, finished)


def project_kernel(me, heads, weight, *outs):
    parts, steps, rows, width = heads.shape
    shares = len(OFFSETS)
    share = weight.shape[1] // shares
    lines = heads[...].reshape(parts * steps * rows, width)
    for at in range(0, shares, 2):
        columns = [
            weight[:, pl.ds(pl.multiple_of((me[0] + OFFSETS[at + i]) % shares * share, share), share)]
            for i in range(2)
        ]
        product = jnp.dot(
            lines, jnp.concatenate(columns, 1), preferred_element_type=jnp.float32
        ).astype(jnp.bfloat16)
        product = product.reshape(parts, steps, rows, 2 * share)
        for i in range(2):
            for q in range(parts):
                outs[at + i][:, q * rows : (q + 1) * rows, :] = product[
                    q, :, :, i * share : (i + 1) * share
                ]


def project(me, heads, weight):
    parts, steps, rows, width = heads.shape
    columns = weight.shape[1]
    share = columns // len(OFFSETS)
    vmem = pl.BlockSpec(memory_space=pltpu.VMEM)
    block = jax.ShapeDtypeStruct((steps, parts * rows, share), jnp.bfloat16)
    return pl.pallas_call(
        project_kernel,
        out_shape=[block] * len(OFFSETS),
        in_specs=[pl.BlockSpec(memory_space=pltpu.SMEM), vmem, vmem],
        out_specs=[vmem] * len(OFFSETS),
        compiler_params=pltpu.CompilerParams(vmem_limit_bytes=32 << 20),
        cost_estimate=pl.CostEstimate(
            flops=2 * parts * steps * rows * width * columns,
            bytes_accessed=6 << 20,
            transcendentals=0,
        ),
        name="project",
    )(me, heads, weight)


def sum_over_ring(blocks):
    size = lax.axis_size("tp")

    def shift(block, by):
        return lax.ppermute(block, "tp", [(i, (i + by) % size) for i in range(size)])

    def total(*terms):
        return sum(term.astype(jnp.float32) for term in terms)

    half = blocks[4].shape[0] // 2
    far_up = shift(blocks[4][:half], 2)
    far_down = shift(blocks[4][half:], -2)
    up, down = shift(blocks[3], 1), shift(blocks[-3], -1)
    near_up, near_down = shift(blocks[1], 1), shift(blocks[-1], -1)
    above = total(blocks[2], up)
    above = jnp.concatenate([above[:half] + far_up.astype(jnp.float32), above[half:]], 0)
    below = total(blocks[-2], down)
    below = jnp.concatenate([below[:half], below[half:] + far_down.astype(jnp.float32)], 0)
    above = shift(above.astype(jnp.bfloat16), 2)
    below = shift(below.astype(jnp.bfloat16), -2)
    return total(blocks[0], near_up, near_down, above, below).astype(jnp.bfloat16)


def per_device(
    queries,
    new_token_cache,
    kv_pool,
    block_table,
    context_len,
    out_proj,
    finished_prompt_cache,
    prompt_blocks,
    prompt_tail,
    prompt_owner,
):
    copies = lax.axis_size("seq")
    receivers = lax.axis_size("grp") * copies
    heads = attend(copies, queries, new_token_cache, kv_pool, block_table, context_len)
    gathered = lax.all_to_all(heads, "seq", split_axis=0, concat_axis=0, tiled=True)
    finished, _ = lax.optimization_barrier((finished_prompt_cache, heads))
    packed = pack(receivers, finished, prompt_blocks, prompt_tail, prompt_owner)
    packed, gathered = lax.optimization_barrier((packed, gathered))
    migrated = lax.all_to_all(packed, ("grp", "seq"), split_axis=0, concat_axis=0, tiled=True)
    me = lax.axis_index("tp").reshape(1)
    decoded = sum_over_ring(dict(zip(OFFSETS, project(me, gathered, out_proj))))
    return (decoded, migrated)


def solution(mesh):
    placed = (
        P(None, ("grp", "seq"), "tp"),
        P(None, ("grp", "seq"), "tp"),
        P(("grp", "seq"), None, "tp"),
        P(("grp", "seq"), None),
        P(("grp", "seq"), None),
        P("tp", "seq"),
        P(("grp", "seq"), None, "tp"),
        P(("grp", "seq"), None),
        P(("grp", "seq"), None),
        P(("grp", "seq"), None),
    )
    return jax.shard_map(
        per_device,
        mesh=mesh,
        in_specs=placed,
        out_specs=(P(None, "grp", ("seq", "tp")), P(("grp", "seq"), None, "tp")),
        check_vma=False,
    )
```

time: 144 us -> 109 us (0.76)
  the two profiles are of different devices: /device:TPU:1 before, /device:TPU:10 now
where the time goes in v1:
time: 109 us
  starting transfers between devices  47.3 us (43%)
  waiting for transfers between devices  40.8 us (37%)
  Pallas kernels  9.98 us (9%)
  local copies, waits for them, and re-layouts  8.48 us (8%)
  other arithmetic  1.1 us (1%)
    ppermute x8, starting transfers between devices, shift(): lax.ppermute(block, 'tp', [(i, (i + by) % size) for i in range(size)])  27.9 us
    all_to_all x1, waiting for transfers between devices, per_device(): lax.all_to_all(heads, 'seq', split_axis=0, concat_axis=0, tiled=True)  22.5 us
    ppermute x8, waiting for transfers between devices, shift(): lax.ppermute(block, 'tp', [(i, (i + by) % size) for i in range(size)])  18.3 us
    all_to_all x1, starting transfers between devices, per_device(): lax.all_to_all(packed, ('grp', 'seq'), split_axis=0, concat_axis=0, tiled...  12.6 us
    unnamed x21, local copies, waits for them, and re-layouts  8.42 us
    all_to_all x1, starting transfers between devices, per_device(): lax.all_to_all(heads, 'seq', split_axis=0, concat_axis=0, tiled=True)  6.77 us
    pallas_call x1, Pallas kernels, attend(): pl.pallas_call(attend_kernel, out_shape=jax.ShapeDtypeStruct((copies, ste...  5.29 us
    pallas_call x1, Pallas kernels, project(): pl.pallas_call(project_kernel, out_shape=[block] * len(OFFSETS), in_specs...  2.39 us
  transfers between devices with their start and end apart: 10, of which 4 were waited for; matrix products, arithmetic and copies ran while one was open for 1% of the time, Pallas kernels for 4%

profile of v1, /device:TPU:10, one launch (start us, length us, event | category | flops | bytes accessed | tf_op | source)
XLA Modules:
  0.0 108.5 jit_solution(10289125246886949358)
XLA Ops:
  0.6 0.0 copy-start
  0.6 1.0 copy-done
  1.7 0.0 copy-start.2
  1.7 0.9 copy-done.2
  2.6 0.0 copy-start.3
  2.6 0.8 copy-done.3
  3.5 0.0 copy-start.4
  3.5 0.7 copy-done.4
  4.1 0.0 copy-start.5
  4.1 0.7 copy-done.5
  4.8 5.3 %attend.1 = bf16[8,4,32,1024]{3,2,1,0:T(8,128)(2,1)} custom-call(s32[2,32]{1,0:T(2,128)S(1)} %bitcast.2, s32[1,32]{1,0:T(1,128)S(1)} %copy-done.5, bf16[4,32,1024]{2,1,0:T(8,128)(2,1)S(1)} %copy-done.2, bf16[4,32,256]{2,1,0:T(8,128)(2,1)S(1)} %copy-done.3, bf16[64,16,256]{2,1,0:T(8,128)(2,1)S(1)} %copy-done), custom_call_target="tpu_custom_call" | custom-call | flops 301989888 | bytes 4194304 | tf_op jit(solution)/shard_map/attend/pallas_call | solution.py:113
  10.1 0.0 copy-start.1
  10.1 0.0 copy-start.6
  10.1 0.0 copy-start.7
  10.1 0.0 copy-start.8
  10.1 6.8 %all-to-all-start = ((bf16[8,4,32,1024]{3,2,1,0:T(8,128)(2,1)}), bf16[8,4,32,1024]{3,2,1,0:T(8,128)(2,1)S(1)}, u32[]{:S(2)}, u32[]{:S(2)}) async-start(bf16[8,4,32,1024]{3,2,1,0:T(8,128)(2,1)} %attend.1), calls=%async_computation | async-start | bytes 4194304 | tf_op jit(solution)/shard_map/all_to_all | solution.py:249
  16.9 0.0 copy-done.1
  16.9 0.0 copy-done.6
  16.9 0.0 copy-done.7
  16.9 0.0 copy-done.8
  16.9 2.3 %pack.1 = bf16[192,16,256]{2,1,0:T(8,128)(2,1)} custom-call(s32[1,32]{1,0:T(1,128)S(1)} %copy-done.6, s32[1,32]{1,0:T(1,128)S(1)} %copy-done.7, s32[1,32]{1,0:T(1,128)S(1)} %copy-done.8, bf16[64,16,256]{2,1,0:T(8,128)(2,1)S(1)} %copy-done.1), custom_call_target="tpu_custom_call" | custom-call | bytes 2097152 | tf_op jit(solution)/shard_map/pack/pallas_call | solution.py:158
  19.2 22.5 %all-to-all-done.heads = bf16[8,4,32,1024]{3,2,1,0:T(8,128)(2,1)S(1)} async-done(((bf16[8,4,32,1024]{3,2,1,0:T(8,128)(2,1)}), bf16[8,4,32,1024]{3,2,1,0:T(8,128)(2,1)S(1)}, u32[]{:S(2)}, u32[]{:S(2)}) %all-to-all-start) | async-done | bytes 2097184 | tf_op jit(solution)/shard_map/all_to_all | solution.py:249
  41.8 12.6 %all-to-all-start.1 = ((bf16[192,16,256]{2,1,0:T(8,128)(2,1)}), bf16[192,16,256]{2,1,0:T(8,128)(2,1)}, u32[]{:S(2)}, u32[]{:S(2)}) async-start(bf16[192,16,256]{2,1,0:T(8,128)(2,1)} %pack.1), calls=%async_computation.1 | async-start | bytes 3145728 | tf_op jit(solution)/shard_map/all_to_all | solution.py:253
  54.4 0.0 copy-start.9
  54.4 1.6 %copy-done.9 = bf16[1024,1024]{1,0:T(8,128)(2,1)S(1)} copy-done((bf16[1024,1024]{1,0:T(8,128)(2,1)S(1)}, bf16[1024,1024]{1,0:T(8,128)(2,1)}, u32[]{:S(2)}) %copy-start.9) | copy-done | bytes 2097176
  56.0 2.4 %project.1 = (bf16[4,256,128]{2,1,0:T(8,128)(2,1)S(1)}, bf16[4,256,128]{2,1,0:T(8,128)(2,1)S(1)}, bf16[4,256,128]{2,1,0:T(8,128)(2,1)S(1)}, bf16[4,256,128]{2,1,...) custom-call(s32[1]{0:T(128)} %bitcast.me, ...), custom_call_target="tpu_custom_call" | custom-call | flops 2147483648 | bytes 6291456 | tf_op jit(solution)/shard_map/project/pallas_call | solution.py:196
  58.4 3.5 %collective-permute-start.2 = (bf16[4,256,128]{2,1,0:T(8,128)(2,1)S(1)}, bf16[4,256,128]{2,1,0:T(8,128)(2,1)S(1)}, u32[]{:S(2)}, u32[]{:S(2)}) collective-permute-start(bf16[4,256,128]{2,1,0:T(8,128)(2,1)S(1)} %get-tuple-element.19), channel_id=1, source_target_pairs={{0,1},{1,2},{2,3},{3,4},{4,5},{5,6},{6,7},{7,0},{8,9},{9,10},{10,1... | collective-permute-start | bytes 786440 | tf_op jit(solution)/shard_map/ppermute | solution.py:215
  61.9 5.7 %collective-permute-start.3 = (bf16[2,256,128]{2,1,0:T(8,128)(2,1)S(1)}, bf16[2,256,128]{2,1,0:T(8,128)(2,1)S(1)}, u32[]{:S(2)}, u32[]{:S(2)}) collective-permute-start(bf16[2,256,128]{2,1,0:T(8,128)(2,1)S(1)} %get-tuple-element.24), channel_id=1, source_target_pairs={{0,2},{1,3},{2,4},{3,5},{4,6},{5,7},{6,0},{7,1},{8,10},{9,11},{10,... | collective-permute-start | bytes 393224 | tf_op jit(solution)/shard_map/ppermute | solution.py:215
  67.7 2.2 %collective-permute-start.6 = (bf16[2,256,128]{2,1,0:T(8,128)(2,1)S(1)}, bf16[2,256,128]{2,1,0:T(8,128)(2,1)S(1)}, u32[]{:S(2)}, u32[]{:S(2)}) collective-permute-start(bf16[2,256,128]{2,1,0:T(8,128)(2,1)S(1)} %get-tuple-element.25), channel_id=1, source_target_pairs={{0,6},{1,7},{2,0},{3,1},{4,2},{5,3},{6,4},{7,5},{8,14},{9,15},{10,... | collective-permute-start | bytes 393224 | tf_op jit(solution)/shard_map/ppermute | solution.py:215
  69.9 2.3 %collective-permute-start = (bf16[4,256,128]{2,1,0:T(8,128)(2,1)S(1)}, bf16[4,256,128]{2,1,0:T(8,128)(2,1)S(1)}, u32[]{:S(2)}, u32[]{:S(2)}) collective-permute-start(bf16[4,256,128]{2,1,0:T(8,128)(2,1)S(1)} %get-tuple-element.16), channel_id=1, source_target_pairs={{0,1},{1,2},{2,3},{3,4},{4,5},{5,6},{6,7},{7,0},{8,9},{9,10},{10,1... | collective-permute-start | bytes 786440 | tf_op jit(solution)/shard_map/ppermute | solution.py:215
  72.2 3.5 %collective-permute-start.1 = (bf16[4,256,128]{2,1,0:T(8,128)(2,1)S(1)}, bf16[4,256,128]{2,1,0:T(8,128)(2,1)S(1)}, u32[]{:S(2)}, u32[]{:S(2)}) collective-permute-start(bf16[4,256,128]{2,1,0:T(8,128)(2,1)S(1)} %get-tuple-element.17), channel_id=1, source_target_pairs={{0,7},{1,0},{2,1},{3,2},{4,3},{5,4},{6,5},{7,6},{8,15},{9,8},{10,9... | collective-permute-start | bytes 786440 | tf_op jit(solution)/shard_map/ppermute | solution.py:215
  75.8 0.0 collective-permute-done.2
  75.8 3.6 %collective-permute-start.5 = (bf16[4,256,128]{2,1,0:T(8,128)(2,1)S(1)}, bf16[4,256,128]{2,1,0:T(8,128)(2,1)S(1)}, u32[]{:S(2)}, u32[]{:S(2)}) collective-permute-start(bf16[4,256,128]{2,1,0:T(8,128)(2,1)S(1)} %get-tuple-element.22), channel_id=1, source_target_pairs={{0,7},{1,0},{2,1},{3,2},{4,3},{5,4},{6,5},{7,6},{8,15},{9,8},{10,9... | collective-permute-start | bytes 786440 | tf_op jit(solution)/shard_map/ppermute | solution.py:215
  79.4 0.1 convert_add_fusion.1
  79.5 0.0 collective-permute-done.3
  79.5 2.9 %collective-permute-start.4 = (bf16[4,256,128]{2,1,0:T(8,128)(2,1)S(1)}, bf16[4,256,128]{2,1,0:T(8,128)(2,1)S(1)}, u32[]{:S(2)}, u32[]{:S(2)}) collective-permute-start(bf16[4,256,128]{2,1,0:T(8,128)(2,1)S(1)} %pad_maximum_fusion), channel_id=1, source_target_pairs={{0,2},{1,3},{2,4},{3,5},{4,6},{5,7},{6,0},{7,1},{8,10},{9,11},{10,... | collective-permute-start | bytes 786440 | tf_op jit(solution)/shard_map/ppermute | solution.py:215
  82.4 6.4 %collective-permute-done.5 = bf16[4,256,128]{2,1,0:T(8,128)(2,1)S(1)} collective-permute-done((bf16[4,256,128]{2,1,0:T(8,128)(2,1)S(1)}, bf16[4,256,128]{2,1,0:T(8,128)(2,1)S(1)}, u32[]{:S(2)}, u32[]{:S(2)}) %collective-permute-start.5) | collective-permute-done | bytes 262176 | tf_op jit(solution)/shard_map/ppermute | solution.py:215
  88.9 0.1 convert_add_fusion
  88.9 0.0 collective-permute-done.6
  89.0 4.1 %collective-permute-start.7 = (bf16[4,256,128]{2,1,0:T(8,128)(2,1)S(1)}, bf16[4,256,128]{2,1,0:T(8,128)(2,1)S(1)}, u32[]{:S(2)}, u32[]{:S(2)}) collective-permute-start(bf16[4,256,128]{2,1,0:T(8,128)(2,1)S(1)} %pad_maximum_fusion.1), channel_id=1, source_target_pairs={{0,6},{1,7},{2,0},{3,1},{4,2},{5,3},{6,4},{7,5},{8,14},{9,15},{10,... | collective-permute-start | bytes 786440 | tf_op jit(solution)/shard_map/ppermute | solution.py:215
  93.2 0.0 collective-permute-done
  93.2 0.0 collective-permute-done.1
  93.2 2.4 %collective-permute-done.4 = bf16[4,256,128]{2,1,0:T(8,128)(2,1)S(1)} collective-permute-done((bf16[4,256,128]{2,1,0:T(8,128)(2,1)S(1)}, bf16[4,256,128]{2,1,0:T(8,128)(2,1)S(1)}, u32[]{:S(2)}, u32[]{:S(2)}) %collective-permute-start.4) | collective-permute-done | bytes 262176 | tf_op jit(solution)/shard_map/ppermute | solution.py:215
  95.6 9.4 %collective-permute-done.7 = bf16[4,256,128]{2,1,0:T(8,128)(2,1)S(1)} collective-permute-done((bf16[4,256,128]{2,1,0:T(8,128)(2,1)S(1)}, bf16[4,256,128]{2,1,0:T(8,128)(2,1)S(1)}, u32[]{:S(2)}, u32[]{:S(2)}) %collective-permute-start.7) | collective-permute-done | bytes 262176 | tf_op jit(solution)/shard_map/ppermute | solution.py:215
  105.0 0.9 add_convert_fusion
  105.9 0.0 all-to-all-done.1
  105.9 2.7 %copy.13 = bf16[192,16,256]{2,1,0:T(8,128)(2,1)} copy(bf16[192,16,256]{2,1,0:T(8,128)(2,1)} %all-to-all-done.1) | data formatting | bytes 3145728
  (7 shorter events, 0.2 us)
Async XLA Ops:
  0.6 1.0 copy-start
  1.7 0.9 copy-start.2
  2.6 0.8 copy-start.3
  3.5 0.7 copy-start.4
  4.1 0.7 copy-start.5
  10.1 6.8 %copy-start.1 = (bf16[64,16,256]{2,1,0:T(8,128)(2,1)S(1)}, bf16[64,16,256]{2,1,0:T(8,128)(2,1)}, u32[]{:S(2)}) copy-start(bf16[64,16,256]{2,1,0:T(8,128)(2,1)} %finished) | copy-start | bytes 1572868
  10.1 6.8 %copy-start.6 = (s32[1,32]{1,0:T(1,128)S(1)}, s32[1,32]{1,0:T(1,128)}, u32[]{:S(2)}) copy-start(s32[1,32]{1,0:T(1,128)} %blocks.1) | copy-start | bytes 388
  10.1 6.8 %copy-start.7 = (s32[1,32]{1,0:T(1,128)S(1)}, s32[1,32]{1,0:T(1,128)}, u32[]{:S(2)}) copy-start(s32[1,32]{1,0:T(1,128)} %tail.1) | copy-start | bytes 388
  10.1 6.8 %copy-start.8 = (s32[1,32]{1,0:T(1,128)S(1)}, s32[1,32]{1,0:T(1,128)}, u32[]{:S(2)}) copy-start(s32[1,32]{1,0:T(1,128)} %owner.1) | copy-start | bytes 388
  10.1 31.6 %all-to-all-start = ((bf16[8,4,32,1024]{3,2,1,0:T(8,128)(2,1)}), bf16[8,4,32,1024]{3,2,1,0:T(8,128)(2,1)S(1)}, u32[]{:S(2)}, u32[]{:S(2)}) async-start(bf16[8,4,32,1024]{3,2,1,0:T(8,128)(2,1)} %attend.1), calls=%async_computation | async-start | bytes 4194304 | tf_op jit(solution)/shard_map/all_to_all | solution.py:249
  41.8 64.1 %all-to-all-start.1 = ((bf16[192,16,256]{2,1,0:T(8,128)(2,1)}), bf16[192,16,256]{2,1,0:T(8,128)(2,1)}, u32[]{:S(2)}, u32[]{:S(2)}) async-start(bf16[192,16,256]{2,1,0:T(8,128)(2,1)} %pack.1), calls=%async_computation.1 | async-start | bytes 3145728 | tf_op jit(solution)/shard_map/all_to_all | solution.py:253
  54.4 1.6 %copy-start.9 = (bf16[1024,1024]{1,0:T(8,128)(2,1)S(1)}, bf16[1024,1024]{1,0:T(8,128)(2,1)}, u32[]{:S(2)}) copy-start(bf16[1024,1024]{1,0:T(8,128)(2,1)} %weight.1) | copy-start | bytes 6291460
  58.4 17.3 %collective-permute-start.2 = (bf16[4,256,128]{2,1,0:T(8,128)(2,1)S(1)}, bf16[4,256,128]{2,1,0:T(8,128)(2,1)S(1)}, u32[]{:S(2)}, u32[]{:S(2)}) collective-permute-start(bf16[4,256,128]{2,1,0:T(8,128)(2,1)S(1)} %get-tuple-element.19), channel_id=1, source_target_pairs={{0,1},{1,2},{2,3},{3,4},{4,5},{5,6},{6,7},{7,0},{8,9},{9,10},{10,1... | collective-permute-start | bytes 786440 | tf_op jit(solution)/shard_map/ppermute | solution.py:215
  61.9 17.5 %collective-permute-start.3 = (bf16[2,256,128]{2,1,0:T(8,128)(2,1)S(1)}, bf16[2,256,128]{2,1,0:T(8,128)(2,1)S(1)}, u32[]{:S(2)}, u32[]{:S(2)}) collective-permute-start(bf16[2,256,128]{2,1,0:T(8,128)(2,1)S(1)} %get-tuple-element.24), channel_id=1, source_target_pairs={{0,2},{1,3},{2,4},{3,5},{4,6},{5,7},{6,0},{7,1},{8,10},{9,11},{10,... | collective-permute-start | bytes 393224 | tf_op jit(solution)/shard_map/ppermute | solution.py:215
  67.7 21.3 %collective-permute-start.6 = (bf16[2,256,128]{2,1,0:T(8,128)(2,1)S(1)}, bf16[2,256,128]{2,1,0:T(8,128)(2,1)S(1)}, u32[]{:S(2)}, u32[]{:S(2)}) collective-permute-start(bf16[2,256,128]{2,1,0:T(8,128)(2,1)S(1)} %get-tuple-element.25), channel_id=1, source_target_pairs={{0,6},{1,7},{2,0},{3,1},{4,2},{5,3},{6,4},{7,5},{8,14},{9,15},{10,... | collective-permute-start | bytes 393224 | tf_op jit(solution)/shard_map/ppermute | solution.py:215
  69.9 23.2 %collective-permute-start = (bf16[4,256,128]{2,1,0:T(8,128)(2,1)S(1)}, bf16[4,256,128]{2,1,0:T(8,128)(2,1)S(1)}, u32[]{:S(2)}, u32[]{:S(2)}) collective-permute-start(bf16[4,256,128]{2,1,0:T(8,128)(2,1)S(1)} %get-tuple-element.16), channel_id=1, source_target_pairs={{0,1},{1,2},{2,3},{3,4},{4,5},{5,6},{6,7},{7,0},{8,9},{9,10},{10,1... | collective-permute-start | bytes 786440 | tf_op jit(solution)/shard_map/ppermute | solution.py:215
  72.2 21.0 %collective-permute-start.1 = (bf16[4,256,128]{2,1,0:T(8,128)(2,1)S(1)}, bf16[4,256,128]{2,1,0:T(8,128)(2,1)S(1)}, u32[]{:S(2)}, u32[]{:S(2)}) collective-permute-start(bf16[4,256,128]{2,1,0:T(8,128)(2,1)S(1)} %get-tuple-element.17), channel_id=1, source_target_pairs={{0,7},{1,0},{2,1},{3,2},{4,3},{5,4},{6,5},{7,6},{8,15},{9,8},{10,9... | collective-permute-start | bytes 786440 | tf_op jit(solution)/shard_map/ppermute | solution.py:215
  75.8 13.1 %collective-permute-start.5 = (bf16[4,256,128]{2,1,0:T(8,128)(2,1)S(1)}, bf16[4,256,128]{2,1,0:T(8,128)(2,1)S(1)}, u32[]{:S(2)}, u32[]{:S(2)}) collective-permute-start(bf16[4,256,128]{2,1,0:T(8,128)(2,1)S(1)} %get-tuple-element.22), channel_id=1, source_target_pairs={{0,7},{1,0},{2,1},{3,2},{4,3},{5,4},{6,5},{7,6},{8,15},{9,8},{10,9... | collective-permute-start | bytes 786440 | tf_op jit(solution)/shard_map/ppermute | solution.py:215
  79.5 16.0 %collective-permute-start.4 = (bf16[4,256,128]{2,1,0:T(8,128)(2,1)S(1)}, bf16[4,256,128]{2,1,0:T(8,128)(2,1)S(1)}, u32[]{:S(2)}, u32[]{:S(2)}) collective-permute-start(bf16[4,256,128]{2,1,0:T(8,128)(2,1)S(1)} %pad_maximum_fusion), channel_id=1, source_target_pairs={{0,2},{1,3},{2,4},{3,5},{4,6},{5,7},{6,0},{7,1},{8,10},{9,11},{10,... | collective-permute-start | bytes 786440 | tf_op jit(solution)/shard_map/ppermute | solution.py:215
  89.0 16.0 %collective-permute-start.7 = (bf16[4,256,128]{2,1,0:T(8,128)(2,1)S(1)}, bf16[4,256,128]{2,1,0:T(8,128)(2,1)S(1)}, u32[]{:S(2)}, u32[]{:S(2)}) collective-permute-start(bf16[4,256,128]{2,1,0:T(8,128)(2,1)S(1)} %pad_maximum_fusion.1), channel_id=1, source_target_pairs={{0,6},{1,7},{2,0},{3,1},{4,2},{5,3},{6,4},{7,5},{8,14},{9,15},{10,... | collective-permute-start | bytes 786440 | tf_op jit(solution)/shard_map/ppermute | solution.py:215

commit v2 on v1

v2 whole, which is shorter than its diff:
```python
import jax
import jax.numpy as jnp
from jax import lax
from jax.experimental import pallas as pl
from jax.experimental.pallas import tpu as pltpu
from jax.sharding import PartitionSpec as P

HEAD_SIZE = 128
PAGE_TOKENS = 16
CAP = 3
NEGATIVE = -1e30
OFFSETS = (4, 3, -3, 2, -2, 1, -1, 0)
PROJECT_WEIGHT = 10
GROUP = 16


def start_all(copies, arrived):
    started = [
        pltpu.make_async_copy(source, target, arrived.at[i])
        for i, (source, target) in enumerate(copies)
    ]
    for copy in started:
        copy.start()
    return started


def pack_blocks(blocks, tail, owner, finished, packed):
    count = finished.shape[0]
    token = lax.broadcasted_iota(jnp.int32, finished.shape[1:], 0)
    start = jnp.int32(0)
    for j in range(blocks.shape[1]):
        held = blocks[0, j]
        for slot in range(CAP):
            valid = jnp.where(slot == held - 1, tail[0, j], PAGE_TOKENS)
            valid = jnp.where(slot < held, valid, 0)
            block = finished[jnp.minimum(start + slot, count - 1)]
            packed[owner[0, j] * CAP + slot] = jnp.where(
                token < valid, block, jnp.zeros_like(block)
            )
        start = start + held


def attend_kernel(
    blocks_hbm,
    tail_hbm,
    owner_hbm,
    finished_hbm,
    table_hbm,
    length_hbm,
    pool_hbm,
    fresh_hbm,
    queries_hbm,
    out,
    packed_hbm,
    blocks,
    tail,
    owner,
    finished,
    table,
    length,
    pool,
    fresh,
    queries,
    packed,
    key_rows,
    value_rows,
    arrived,
    left,
):
    sources = (blocks_hbm, tail_hbm, owner_hbm, finished_hbm)
    sources += (table_hbm, length_hbm, pool_hbm, fresh_hbm, queries_hbm)
    targets = (blocks, tail, owner, finished, table, length, pool, fresh, queries)
    loads = start_all(list(zip(sources, targets)), arrived)
    packed[...] = jnp.zeros_like(packed)
    steps, rows, width = queries.shape
    heads = width // HEAD_SIZE
    pages = table.shape[0]
    context = pages * PAGE_TOKENS
    cached = GROUP * context
    recent = steps * GROUP
    scale = HEAD_SIZE ** (-0.5)

    def index(columns, axis):
        return lax.broadcasted_iota(jnp.int32, (GROUP, columns), axis)

    own_cached = index(cached, 1) // context == index(cached, 0)
    cached_place = index(cached, 1) % context
    own_recent = index(recent, 1) % GROUP == index(recent, 0)
    recent_bias = [
        jnp.where(own_recent & (index(recent, 1) // GROUP <= s), 0.0, NEGATIVE)
        for s in range(steps)
    ]
    tile_row = index(cached, 0)
    for load in loads:
        load.wait()
    pack_blocks(blocks, tail, owner, finished, packed)
    (store,) = start_all([(packed, packed_hbm)], left)
    groups = range(rows // GROUP)
    cached_bias = []
    for g in groups:
        first = g * GROUP
        limit = jnp.zeros((GROUP, cached), jnp.int32)
        for r in range(GROUP):
            limit = jnp.where(tile_row == r, length[0, first + r], limit)
            for j in range(pages):
                page = pool[table[j, first + r]]
                at = pl.ds(r * context + j * PAGE_TOKENS, PAGE_TOKENS)
                key_rows[g, at, :] = page[:, :HEAD_SIZE]
                value_rows[g, at, :] = page[:, HEAD_SIZE:]
        for u in range(steps):
            token = fresh[u, pl.ds(first, GROUP), :]
            at = pl.ds(cached + u * GROUP, GROUP)
            key_rows[g, at, :] = token[:, :HEAD_SIZE]
            value_rows[g, at, :] = token[:, HEAD_SIZE:]
        cached_bias.append(jnp.where(own_cached & (cached_place < limit), 0.0, NEGATIVE))
    for g in groups:
        at = pl.ds(g * GROUP, GROUP)
        scores = []
        for s in range(steps):
            query = jnp.concatenate(
                [queries[s, at, h * HEAD_SIZE : (h + 1) * HEAD_SIZE] for h in range(heads)], 0
            )
            scores.append(
                lax.dot_general(
                    query,
                    key_rows[g],
                    (((1,), (1,)), ((), ())),
                    preferred_element_type=jnp.float32,
                )
            )
        probs = []
        for s in range(steps):
            bias = jnp.concatenate([cached_bias[g], recent_bias[s]], 1)
            masked = scores[s].reshape(heads, GROUP, cached + recent) * scale + bias[None]
            raw = jnp.exp(masked - jnp.max(masked, -1, keepdims=True))
            share = raw * (1.0 / jnp.sum(raw, -1, keepdims=True))
            probs.append(share.astype(jnp.bfloat16).reshape(heads * GROUP, cached + recent))
        for s in range(steps):
            mixed = jnp.dot(probs[s], value_rows[g], preferred_element_type=jnp.float32)
            mixed = mixed.astype(jnp.bfloat16)
            for h in range(heads):
                out[s, at, h * HEAD_SIZE : (h + 1) * HEAD_SIZE] = mixed[h * GROUP : (h + 1) * GROUP]
    store.wait()


def attend_and_pack(receivers, queries, fresh, pool, table, length, finished, blocks, tail, owner):
    steps, rows, width = queries.shape
    table = table.T
    keys = GROUP * (table.shape[0] * PAGE_TOKENS + steps)
    operands = (blocks, tail, owner, finished, table, length, pool, fresh, queries)
    far = pl.BlockSpec(memory_space=pltpu.HBM)
    packed = (receivers * CAP,) + finished.shape[1:]
    return pl.pallas_call(
        attend_kernel,
        out_shape=[
            jax.ShapeDtypeStruct(queries.shape, jnp.bfloat16),
            jax.ShapeDtypeStruct(packed, finished.dtype),
        ],
        in_specs=[far] * len(operands),
        out_specs=[pl.BlockSpec(memory_space=pltpu.VMEM), far],
        scratch_shapes=[
            pltpu.SMEM(operand.shape, operand.dtype)
            if operand.dtype == jnp.int32
            else pltpu.VMEM(operand.shape, operand.dtype)
            for operand in operands
        ]
        + [
            pltpu.VMEM(packed, finished.dtype),
            pltpu.VMEM((rows // GROUP, keys, HEAD_SIZE), jnp.bfloat16),
            pltpu.VMEM((rows // GROUP, keys, HEAD_SIZE), jnp.bfloat16),
            pltpu.SemaphoreType.DMA((len(operands),)),
            pltpu.SemaphoreType.DMA((1,)),
        ],
        compiler_params=pltpu.CompilerParams(vmem_limit_bytes=60 << 20),
        cost_estimate=pl.CostEstimate(
            flops=4 * steps * rows * (width // HEAD_SIZE) * keys * HEAD_SIZE,
            bytes_accessed=5 << 20,
            transcendentals=0,
        ),
        name="attend_and_pack",
    )(*operands)


def project_kernel(me, place, *refs):
    parts = refs[: -1 - len(OFFSETS)]
    weight = refs[len(parts)]
    outs = refs[len(parts) + 1 :]
    steps, rows, width = parts[0].shape
    shares = len(OFFSETS)
    share = weight.shape[1] // shares
    lines = jnp.concatenate([part[...].reshape(steps * rows, width) for part in parts], 0)
    for at in range(0, shares, 2):
        columns = [
            weight[:, pl.ds(pl.multiple_of((me[0] + OFFSETS[at + i]) % shares * share, share), share)]
            for i in range(2)
        ]
        product = jnp.dot(
            lines, jnp.concatenate(columns, 1), preferred_element_type=jnp.float32
        ).astype(jnp.bfloat16)
        product = product.reshape(len(parts), steps, rows, 2 * share)
        for q in range(len(parts)):
            to = pl.ds(pl.multiple_of(place[q] * rows, rows), rows)
            for i in range(2):
                outs[at + i][:, to, :] = product[q, :, :, i * share : (i + 1) * share]


def project(me, place, parts, weight):
    steps, rows, width = parts[0].shape
    columns = weight.shape[1]
    share = columns // len(OFFSETS)
    smem = pl.BlockSpec(memory_space=pltpu.SMEM)
    vmem = pl.BlockSpec(memory_space=pltpu.VMEM)
    block = jax.ShapeDtypeStruct((steps, len(parts) * rows, share), jnp.bfloat16)
    return pl.pallas_call(
        project_kernel,
        out_shape=[block] * len(OFFSETS),
        in_specs=[smem, smem] + [vmem] * (len(parts) + 1),
        out_specs=[vmem] * len(OFFSETS),
        compiler_params=pltpu.CompilerParams(vmem_limit_bytes=32 << 20),
        cost_estimate=pl.CostEstimate(
            flops=PROJECT_WEIGHT * 2 * len(parts) * steps * rows * width * columns,
            bytes_accessed=6 << 20,
            transcendentals=0,
        ),
        name="project",
    )(me, place, *parts, weight)


def gather_heads(heads):
    across, along = 2, lax.axis_size("seq") // 2

    def shift(block, by):
        pairs = [(z * along + x, z * along + (x + by) % along) for z in range(across) for x in range(along)]
        return lax.ppermute(block, "seq", pairs)

    me = lax.axis_index("seq")
    z, x = me // along, me % along
    other = lax.ppermute(heads, "seq", [(i, (i + along) % (2 * along)) for i in range(2 * along)])
    parts, place = [heads, other], [me, (1 - z) * along + x]
    for row, block in ((z, heads), (1 - z, other)):
        for by in (1, -1, 2):
            parts.append(shift(block, by))
            place.append(row * along + (x - by) % along)
    return parts, jnp.stack(place)


def finish_kernel(migrated_hbm, *refs):
    terms, (out, moved_hbm, moved) = refs[:-3], refs[-3:]
    copy = pltpu.make_async_copy(migrated_hbm, moved_hbm, moved)
    copy.start()
    out[...] = sum(term[...].astype(jnp.float32) for term in terms).astype(out.dtype)
    copy.wait()


def finish(migrated, terms):
    far = pl.BlockSpec(memory_space=pltpu.HBM)
    vmem = pl.BlockSpec(memory_space=pltpu.VMEM)
    return pl.pallas_call(
        finish_kernel,
        out_shape=[
            jax.ShapeDtypeStruct(terms[0].shape, jnp.bfloat16),
            jax.ShapeDtypeStruct(migrated.shape, migrated.dtype),
        ],
        in_specs=[far] + [vmem] * len(terms),
        out_specs=[vmem, far],
        scratch_shapes=[pltpu.SemaphoreType.DMA],
        compiler_params=pltpu.CompilerParams(vmem_limit_bytes=32 << 20),
        cost_estimate=pl.CostEstimate(flops=0, bytes_accessed=4 << 20, transcendentals=0),
        name="finish",
    )(migrated, *terms)


def signs(me):
    return 1 - 2 * (me % 2), 1 - 2 * (me // 2 % 2)


def share_order(me):
    near, next_near = signs(me)
    offsets = (4, 3 * near, -3 * near, 2 * next_near, -2 * next_near, near, -near, 0)
    return jnp.stack([(me + offset) % SHARES for offset in offsets])


def send_round_ring(blocks):
    size = lax.axis_size("tp")

    def shift(block, by):
        return lax.ppermute(block, "tp", [(i, (i + by) % size) for i in range(size)])

    def total(*terms):
        return sum(term.astype(jnp.float32) for term in terms)

    half = blocks[4].shape[0] // 2
    far_up = shift(blocks[4][:half], 2)
    far_down = shift(blocks[4][half:], -2)
    up, down = shift(blocks[3], 1), shift(blocks[-3], -1)
    near_up, near_down = shift(blocks[1], 1), shift(blocks[-1], -1)
    above = total(blocks[2], up)
    above = jnp.concatenate([above[:half] + far_up.astype(jnp.float32), above[half:]], 0)
    below = total(blocks[-2], down)
    below = jnp.concatenate([below[:half], below[half:] + far_down.astype(jnp.float32)], 0)
    above = shift(above.astype(jnp.bfloat16), 2)
    below = shift(below.astype(jnp.bfloat16), -2)
    return blocks[0], near_up, near_down, above, below


def per_device(
    queries,
    new_token_cache,
    kv_pool,
    block_table,
    context_len,
    out_proj,
    finished_prompt_cache,
    prompt_blocks,
    prompt_tail,
    prompt_owner,
):
    receivers = lax.axis_size("grp") * lax.axis_size("seq")
    heads, packed = attend_and_pack(
        receivers,
        queries,
        new_token_cache,
        kv_pool,
        block_table,
        context_len,
        finished_prompt_cache,
        prompt_blocks,
        prompt_tail,
        prompt_owner,
    )
    parts, place = gather_heads(heads)
    migrated = lax.all_to_all(packed, ("grp", "seq"), split_axis=0, concat_axis=0, tiled=True)
    me = lax.axis_index("tp").reshape(1)
    terms = send_round_ring(dict(zip(OFFSETS, project(me, place, parts, out_proj))))
    decoded, migrated = finish(migrated, terms)
    return (decoded, migrated)


def solution(mesh):
    placed = (
        P(None, ("grp", "seq"), "tp"),
        P(None, ("grp", "seq"), "tp"),
        P(("grp", "seq"), None, "tp"),
        P(("grp", "seq"), None),
        P(("grp", "seq"), None),
        P("tp", "seq"),
        P(("grp", "seq"), None, "tp"),
        P(("grp", "seq"), None),
        P(("grp", "seq"), None),
        P(("grp", "seq"), None),
    )
    return jax.shard_map(
        per_device,
        mesh=mesh,
        in_specs=placed,
        out_specs=(P(None, "grp", ("seq", "tp")), P(("grp", "seq"), None, "tp")),
        check_vma=False,
    )
```

time: 109 us -> 99.1 us (0.909)
  the two profiles are of different devices: /device:TPU:10 before, /device:TPU:26 now
where the time goes in v2:
time: 99.1 us; the launch traced here: 98.4 us
  starting transfers between devices  64.5 us (65%)
  waiting for transfers between devices  19 us (19%)
  Pallas kernels  10.3 us (10%)
  local copies, waits for them, and re-layouts  3.38 us (3%)
  between operations  1.01 us (1%)
    ppermute x8, starting transfers between devices, shift(): lax.ppermute(block, 'tp', [(i, (i + by) % size) for i in range(size)])  27.2 us
    ppermute x6, starting transfers between devices, shift(): return lax.ppermute(block, 'seq', pairs)  20.2 us
    ppermute x8, waiting for transfers between devices, shift(): lax.ppermute(block, 'tp', [(i, (i + by) % size) for i in range(size)])  18.9 us
    all_to_all x1, starting transfers between devices, per_device(): lax.all_to_all(packed, ('grp', 'seq'), split_axis=0, concat_axis=0, tiled...  12.8 us
    pallas_call x1, Pallas kernels, attend_and_pack(): pl.pallas_call(attend_kernel, out_shape=[jax.ShapeDtypeStruct(queries.sha...  5.09 us
    ppermute x1, starting transfers between devices, gather_heads(): lax.ppermute(heads, 'seq', [(i, (i + along) % (2 * along)) for i in range...  4.28 us
    pallas_call x1, Pallas kernels, project(): pl.pallas_call(project_kernel, out_shape=[block] * len(OFFSETS), in_specs...  3.34 us
    unnamed x8, local copies, waits for them, and re-layouts  3.24 us
  transfers between devices with their start and end apart: 16, of which 3 were waited for; matrix products, arithmetic and copies ran while one was open for 0% of the time, Pallas kernels for 3%

profile of v2, /device:TPU:26, one launch (start us, length us, event | category | flops | bytes accessed | tf_op | source)
XLA Modules:
  0.0 98.4 jit_solution(751025872734346279)
XLA Ops:
  0.6 5.1 %attend_and_pack.1 = (bf16[4,32,1024]{2,1,0:T(8,128)(2,1)}, bf16[192,16,256]{2,1,0:T(8,128)(2,1)}) custom-call(s32[1,32]{1,0:T(1,128)} %blocks_hbm.1, s32[1,32]{1,0:T(1,128)} %tail_hbm.1, s32[1,32]{1,0:T(1,128)} %owner_hbm.1, bf16[64,16,256]{2,1,0:T(8,128)(2,1)} %finished_hbm.1, s32[2,32]{1,0:T(2,128)} %bitcast.10, s32[1,32]{1,0:T(1,128)} %length_hbm.1, ...), custom_call_target="tpu_custom_call" | custom-call | flops 301989888 | bytes 5242880 | tf_op jit(solution)/shard_map/attend_and_pack/pallas_call | solution.py:153
  5.7 4.3 %collective-permute-start = (bf16[4,32,1024]{2,1,0:T(8,128)(2,1)}, bf16[4,32,1024]{2,1,0:T(8,128)(2,1)S(1)}, u32[]{:S(2)}, u32[]{:S(2)}) collective-permute-start(bf16[4,32,1024]{2,1,0:T(8,128)(2,1)} %get-tuple-element.13.refs_0_), channel_id=1, source_target_pairs={{0,32},{8,40},{16,48},{24,56},{32,0},{40,8},{48,16},{56,24},{1,33}... | collective-permute-start | bytes 786440 | tf_op jit(solution)/shard_map/ppermute | solution.py:238
  10.0 4.0 %collective-permute-start.3 = (bf16[4,32,1024]{2,1,0:T(8,128)(2,1)}, bf16[4,32,1024]{2,1,0:T(8,128)(2,1)S(1)}, u32[]{:S(2)}, u32[]{:S(2)}) collective-permute-start(bf16[4,32,1024]{2,1,0:T(8,128)(2,1)} %get-tuple-element.13.refs_0_), channel_id=1, source_target_pairs={{0,16},{8,24},{16,0},{24,8},{32,48},{40,56},{48,32},{56,40},{1,17}... | collective-permute-start | bytes 786440 | tf_op jit(solution)/shard_map/ppermute | solution.py:234
  14.1 3.3 %collective-permute-start.2 = (bf16[4,32,1024]{2,1,0:T(8,128)(2,1)}, bf16[4,32,1024]{2,1,0:T(8,128)(2,1)S(1)}, u32[]{:S(2)}, u32[]{:S(2)}) collective-permute-start(bf16[4,32,1024]{2,1,0:T(8,128)(2,1)} %get-tuple-element.13.refs_0_), channel_id=1, source_target_pairs={{0,24},{8,0},{16,8},{24,16},{32,56},{40,32},{48,40},{56,48},{1,25}... | collective-permute-start | bytes 786440 | tf_op jit(solution)/shard_map/ppermute | solution.py:234
  17.4 2.5 %collective-permute-start.1 = (bf16[4,32,1024]{2,1,0:T(8,128)(2,1)}, bf16[4,32,1024]{2,1,0:T(8,128)(2,1)S(1)}, u32[]{:S(2)}, u32[]{:S(2)}) collective-permute-start(bf16[4,32,1024]{2,1,0:T(8,128)(2,1)} %get-tuple-element.13.refs_0_), channel_id=1, source_target_pairs={{0,8},{8,16},{16,24},{24,0},{32,40},{40,48},{48,56},{56,32},{1,9},... | collective-permute-start | bytes 786440 | tf_op jit(solution)/shard_map/ppermute | solution.py:234
  19.9 0.0 collective-permute-done.refs_1_
  19.9 4.5 %collective-permute-start.6 = (bf16[4,32,1024]{2,1,0:T(8,128)(2,1)S(1)}, bf16[4,32,1024]{2,1,0:T(8,128)(2,1)S(1)}, u32[]{:S(2)}, u32[]{:S(2)}) collective-permute-start(bf16[4,32,1024]{2,1,0:T(8,128)(2,1)S(1)} %collective-permute-done.refs_1_), channel_id=1, source_target_pairs={{0,16},{8,24},{16,0},{24,8},{32,48},{40,56},{48,32},{56,40},{1,17}... | collective-permute-start | bytes 786440 | tf_op jit(solution)/shard_map/ppermute | solution.py:234
  24.5 1.9 %collective-permute-start.5 = (bf16[4,32,1024]{2,1,0:T(8,128)(2,1)S(1)}, bf16[4,32,1024]{2,1,0:T(8,128)(2,1)S(1)}, u32[]{:S(2)}, u32[]{:S(2)}) collective-permute-start(bf16[4,32,1024]{2,1,0:T(8,128)(2,1)S(1)} %collective-permute-done.refs_1_), channel_id=1, source_target_pairs={{0,24},{8,0},{16,8},{24,16},{32,56},{40,32},{48,40},{56,48},{1,25}... | collective-permute-start | bytes 786440 | tf_op jit(solution)/shard_map/ppermute | solution.py:234
  26.4 0.0 collective-permute-done.3.refs_4_
  26.4 3.9 %collective-permute-start.4 = (bf16[4,32,1024]{2,1,0:T(8,128)(2,1)S(1)}, bf16[4,32,1024]{2,1,0:T(8,128)(2,1)}, u32[]{:S(2)}, u32[]{:S(2)}) collective-permute-start(bf16[4,32,1024]{2,1,0:T(8,128)(2,1)S(1)} %collective-permute-done.refs_1_), channel_id=1, source_target_pairs={{0,8},{8,16},{16,24},{24,0},{32,40},{40,48},{48,56},{56,32},{1,9},... | collective-permute-start | bytes 786440 | tf_op jit(solution)/shard_map/ppermute | solution.py:234
  30.3 0.0 copy-start.1
  30.3 12.8 %all-to-all-start = ((bf16[192,16,256]{2,1,0:T(8,128)(2,1)}), bf16[192,16,256]{2,1,0:T(8,128)(2,1)S(1)}, u32[]{:S(2)}, u32[]{:S(2)}) async-start(bf16[192,16,256]{2,1,0:T(8,128)(2,1)} %get-tuple-element.12), calls=%async_computation | async-start | bytes 3145728 | tf_op jit(solution)/shard_map/all_to_all | solution.py:332
  43.3 0.1 stack.35.place
  43.3 0.0 collective-permute-done.2.refs_3_
  43.3 0.0 collective-permute-done.1.refs_2_
  43.4 0.0 collective-permute-done.6.refs_7_
  43.4 0.0 collective-permute-done.5.refs_6_
  43.4 0.0 copy-start.2
  43.4 0.7 copy-done.2
  44.1 0.0 collective-permute-done.4.refs_5_
  44.1 0.0 copy-done.1
  44.1 0.0 copy-start
  44.1 1.6 %copy-done = bf16[1024,1024]{1,0:T(8,128)(2,1)S(1)} copy-done((bf16[1024,1024]{1,0:T(8,128)(2,1)S(1)}, bf16[1024,1024]{1,0:T(8,128)(2,1)}, u32[]{:S(2)}) %copy-start) | copy-done | bytes 2097176
  45.7 0.0 copy-start.3
  45.7 0.9 copy-done.3
  46.6 3.3 %project.1 = (bf16[4,256,128]{2,1,0:T(8,128)(2,1)S(1)}, bf16[4,256,128]{2,1,0:T(8,128)(2,1)S(1)}, bf16[4,256,128]{2,1,0:T(8,128)(2,1)S(1)}, bf16[4,256,128]{2,1,...) custom-call(s32[1]{0:T(128)} %bitcast.1.me, ...), custom_call_target="tpu_custom_call" | custom-call | flops 21474836480 | bytes 6291456 | tf_op jit(solution)/shard_map/project/pallas_call | solution.py:214
  50.0 4.7 %collective-permute-start.9 = (bf16[4,256,128]{2,1,0:T(8,128)(2,1)S(1)}, bf16[4,256,128]{2,1,0:T(8,128)(2,1)S(1)}, u32[]{:S(2)}, u32[]{:S(2)}) collective-permute-start(bf16[4,256,128]{2,1,0:T(8,128)(2,1)S(1)} %get-tuple-element.18), channel_id=1, source_target_pairs={{0,1},{1,2},{2,3},{3,4},{4,5},{5,6},{6,7},{7,0},{8,9},{9,10},{10,1... | collective-permute-start | bytes 786440 | tf_op jit(solution)/shard_map/ppermute | solution.py:287
  54.7 1.9 %collective-permute-start.13 = (bf16[2,256,128]{2,1,0:T(8,128)(2,1)S(1)}, bf16[2,256,128]{2,1,0:T(8,128)(2,1)S(1)}, u32[]{:S(2)}, u32[]{:S(2)}) collective-permute-start(bf16[2,256,128]{2,1,0:T(8,128)(2,1)S(1)} %get-tuple-element.22), channel_id=1, source_target_pairs={{0,6},{1,7},{2,0},{3,1},{4,2},{5,3},{6,4},{7,5},{8,14},{9,15},{10,... | collective-permute-start | bytes 393224 | tf_op jit(solution)/shard_map/ppermute | solution.py:287
  56.6 6.0 %collective-permute-start.10 = (bf16[2,256,128]{2,1,0:T(8,128)(2,1)S(1)}, bf16[2,256,128]{2,1,0:T(8,128)(2,1)S(1)}, u32[]{:S(2)}, u32[]{:S(2)}) collective-permute-start(bf16[2,256,128]{2,1,0:T(8,128)(2,1)S(1)} %get-tuple-element.23), channel_id=1, source_target_pairs={{0,2},{1,3},{2,4},{3,5},{4,6},{5,7},{6,0},{7,1},{8,10},{9,11},{10,... | collective-permute-start | bytes 393224 | tf_op jit(solution)/shard_map/ppermute | solution.py:287
  62.7 1.9 %collective-permute-start.7 = (bf16[4,256,128]{2,1,0:T(8,128)(2,1)S(1)}, bf16[4,256,128]{2,1,0:T(8,128)(2,1)S(1)}, u32[]{:S(2)}, u32[]{:S(2)}) collective-permute-start(bf16[4,256,128]{2,1,0:T(8,128)(2,1)S(1)} %get-tuple-element.15), channel_id=1, source_target_pairs={{0,1},{1,2},{2,3},{3,4},{4,5},{5,6},{6,7},{7,0},{8,9},{9,10},{10,1... | collective-permute-start | bytes 786440 | tf_op jit(solution)/shard_map/ppermute | solution.py:287
  64.6 3.9 %collective-permute-start.8 = (bf16[4,256,128]{2,1,0:T(8,128)(2,1)S(1)}, bf16[4,256,128]{2,1,0:T(8,128)(2,1)S(1)}, u32[]{:S(2)}, u32[]{:S(2)}) collective-permute-start(bf16[4,256,128]{2,1,0:T(8,128)(2,1)S(1)} %get-tuple-element.16), channel_id=1, source_target_pairs={{0,7},{1,0},{2,1},{3,2},{4,3},{5,4},{6,5},{7,6},{8,15},{9,8},{10,9... | collective-permute-start | bytes 786440 | tf_op jit(solution)/shard_map/ppermute | solution.py:287
  68.5 0.0 collective-permute-done.9
  68.5 1.9 %collective-permute-start.12 = (bf16[4,256,128]{2,1,0:T(8,128)(2,1)S(1)}, bf16[4,256,128]{2,1,0:T(8,128)(2,1)S(1)}, u32[]{:S(2)}, u32[]{:S(2)}) collective-permute-start(bf16[4,256,128]{2,1,0:T(8,128)(2,1)S(1)} %get-tuple-element.21), channel_id=1, source_target_pairs={{0,7},{1,0},{2,1},{3,2},{4,3},{5,4},{6,5},{7,6},{8,15},{9,8},{10,9... | collective-permute-start | bytes 786440 | tf_op jit(solution)/shard_map/ppermute | solution.py:287
  70.5 0.1 convert_add_fusion.1
  70.6 0.0 collective-permute-done.10
  70.7 4.6 %collective-permute-start.11 = (bf16[4,256,128]{2,1,0:T(8,128)(2,1)S(1)}, bf16[4,256,128]{2,1,0:T(8,128)(2,1)S(1)}, u32[]{:S(2)}, u32[]{:S(2)}) collective-permute-start(bf16[4,256,128]{2,1,0:T(8,128)(2,1)S(1)} %pad_maximum_fusion), channel_id=1, source_target_pairs={{0,2},{1,3},{2,4},{3,5},{4,6},{5,7},{6,0},{7,1},{8,10},{9,11},{10,... | collective-permute-start | bytes 786440 | tf_op jit(solution)/shard_map/ppermute | solution.py:287
  75.2 5.6 %collective-permute-done.12 = bf16[4,256,128]{2,1,0:T(8,128)(2,1)S(1)} collective-permute-done((bf16[4,256,128]{2,1,0:T(8,128)(2,1)S(1)}, bf16[4,256,128]{2,1,0:T(8,128)(2,1)S(1)}, u32[]{:S(2)}, u32[]{:S(2)}) %collective-permute-start.12) | collective-permute-done | bytes 262176 | tf_op jit(solution)/shard_map/ppermute | solution.py:287
  80.9 0.1 convert_add_fusion
  80.9 0.0 collective-permute-done.13
  81.0 2.2 %collective-permute-start.14 = (bf16[4,256,128]{2,1,0:T(8,128)(2,1)S(1)}, bf16[4,256,128]{2,1,0:T(8,128)(2,1)S(1)}, u32[]{:S(2)}, u32[]{:S(2)}) collective-permute-start(bf16[4,256,128]{2,1,0:T(8,128)(2,1)S(1)} %pad_maximum_fusion.1), channel_id=1, source_target_pairs={{0,6},{1,7},{2,0},{3,1},{4,2},{5,3},{6,4},{7,5},{8,14},{9,15},{10,... | collective-permute-start | bytes 786440 | tf_op jit(solution)/shard_map/ppermute | solution.py:287
  83.2 0.0 collective-permute-done.7.refs_1_
  83.2 0.0 collective-permute-done.8.refs_2_
  83.2 2.6 %collective-permute-done.11.refs_3_ = bf16[4,256,128]{2,1,0:T(8,128)(2,1)S(1)} collective-permute-done((bf16[4,256,128]{2,1,0:T(8,128)(2,1)S(1)}, bf16[4,256,128]{2,1,0:T(8,128)(2,1)S(1)}, u32[]{:S(2)}, u32[]{:S(2)}) %collective-permute-start.11) | collective-permute-done | bytes 262176 | tf_op jit(solution)/shard_map/ppermute | solution.py:287
  85.8 10.7 %collective-permute-done.14.refs_4_ = bf16[4,256,128]{2,1,0:T(8,128)(2,1)S(1)} collective-permute-done((bf16[4,256,128]{2,1,0:T(8,128)(2,1)S(1)}, bf16[4,256,128]{2,1,0:T(8,128)(2,1)S(1)}, u32[]{:S(2)}, u32[]{:S(2)}) %collective-permute-start.14) | collective-permute-done | bytes 262176 | tf_op jit(solution)/shard_map/ppermute | solution.py:287
  96.5 0.0 all-to-all-done.migrated_hbm
  96.5 1.9 %finish.1 = (bf16[4,256,128]{2,1,0:T(8,128)(2,1)}, bf16[192,16,256]{2,1,0:T(8,128)(2,1)}) custom-call(bf16[192,16,256]{2,1,0:T(8,128)(2,1)S(1)} %all-to-all-done.migrated_hbm, bf16[4,256,128]{2,1,0:T(8,128)(2,1)S(1)} %get-tuple-element.14.refs_0_, bf16[4,256,128]{2,1,0:T(8,128)(2,1)S(1)} %collective-permute-done.7.refs_1_, ...), custom_call_target="tpu_custom_call" | custom-call | bytes 4194304 | tf_op jit(solution)/shard_map/finish/pallas_call | solution.py:258
  (7 shorter events, 0.2 us)
Async XLA Ops:
  5.7 14.2 %collective-permute-start = (bf16[4,32,1024]{2,1,0:T(8,128)(2,1)}, bf16[4,32,1024]{2,1,0:T(8,128)(2,1)S(1)}, u32[]{:S(2)}, u32[]{:S(2)}) collective-permute-start(bf16[4,32,1024]{2,1,0:T(8,128)(2,1)} %get-tuple-element.13.refs_0_), channel_id=1, source_target_pairs={{0,32},{8,40},{16,48},{24,56},{32,0},{40,8},{48,16},{56,24},{1,33}... | collective-permute-start | bytes 786440 | tf_op jit(solution)/shard_map/ppermute | solution.py:238
  10.0 16.4 %collective-permute-start.3 = (bf16[4,32,1024]{2,1,0:T(8,128)(2,1)}, bf16[4,32,1024]{2,1,0:T(8,128)(2,1)S(1)}, u32[]{:S(2)}, u32[]{:S(2)}) collective-permute-start(bf16[4,32,1024]{2,1,0:T(8,128)(2,1)} %get-tuple-element.13.refs_0_), channel_id=1, source_target_pairs={{0,16},{8,24},{16,0},{24,8},{32,48},{40,56},{48,32},{56,40},{1,17}... | collective-permute-start | bytes 786440 | tf_op jit(solution)/shard_map/ppermute | solution.py:234
  14.1 29.3 %collective-permute-start.2 = (bf16[4,32,1024]{2,1,0:T(8,128)(2,1)}, bf16[4,32,1024]{2,1,0:T(8,128)(2,1)S(1)}, u32[]{:S(2)}, u32[]{:S(2)}) collective-permute-start(bf16[4,32,1024]{2,1,0:T(8,128)(2,1)} %get-tuple-element.13.refs_0_), channel_id=1, source_target_pairs={{0,24},{8,0},{16,8},{24,16},{32,56},{40,32},{48,40},{56,48},{1,25}... | collective-permute-start | bytes 786440 | tf_op jit(solution)/shard_map/ppermute | solution.py:234
  17.4 25.9 %collective-permute-start.1 = (bf16[4,32,1024]{2,1,0:T(8,128)(2,1)}, bf16[4,32,1024]{2,1,0:T(8,128)(2,1)S(1)}, u32[]{:S(2)}, u32[]{:S(2)}) collective-permute-start(bf16[4,32,1024]{2,1,0:T(8,128)(2,1)} %get-tuple-element.13.refs_0_), channel_id=1, source_target_pairs={{0,8},{8,16},{16,24},{24,0},{32,40},{40,48},{48,56},{56,32},{1,9},... | collective-permute-start | bytes 786440 | tf_op jit(solution)/shard_map/ppermute | solution.py:234
  19.9 23.4 %collective-permute-start.6 = (bf16[4,32,1024]{2,1,0:T(8,128)(2,1)S(1)}, bf16[4,32,1024]{2,1,0:T(8,128)(2,1)S(1)}, u32[]{:S(2)}, u32[]{:S(2)}) collective-permute-start(bf16[4,32,1024]{2,1,0:T(8,128)(2,1)S(1)} %collective-permute-done.refs_1_), channel_id=1, source_target_pairs={{0,16},{8,24},{16,0},{24,8},{32,48},{40,56},{48,32},{56,40},{1,17}... | collective-permute-start | bytes 786440 | tf_op jit(solution)/shard_map/ppermute | solution.py:234
  24.5 18.9 %collective-permute-start.5 = (bf16[4,32,1024]{2,1,0:T(8,128)(2,1)S(1)}, bf16[4,32,1024]{2,1,0:T(8,128)(2,1)S(1)}, u32[]{:S(2)}, u32[]{:S(2)}) collective-permute-start(bf16[4,32,1024]{2,1,0:T(8,128)(2,1)S(1)} %collective-permute-done.refs_1_), channel_id=1, source_target_pairs={{0,24},{8,0},{16,8},{24,16},{32,56},{40,32},{48,40},{56,48},{1,25}... | collective-permute-start | bytes 786440 | tf_op jit(solution)/shard_map/ppermute | solution.py:234
  26.4 17.7 %collective-permute-start.4 = (bf16[4,32,1024]{2,1,0:T(8,128)(2,1)S(1)}, bf16[4,32,1024]{2,1,0:T(8,128)(2,1)}, u32[]{:S(2)}, u32[]{:S(2)}) collective-permute-start(bf16[4,32,1024]{2,1,0:T(8,128)(2,1)S(1)} %collective-permute-done.refs_1_), channel_id=1, source_target_pairs={{0,8},{8,16},{16,24},{24,0},{32,40},{40,48},{48,56},{56,32},{1,9},... | collective-permute-start | bytes 786440 | tf_op jit(solution)/shard_map/ppermute | solution.py:234
  30.3 13.8 %copy-start.1 = (bf16[4,32,1024]{2,1,0:T(8,128)(2,1)S(1)}, bf16[4,32,1024]{2,1,0:T(8,128)(2,1)}, u32[]{:S(2)}) copy-start(bf16[4,32,1024]{2,1,0:T(8,128)(2,1)} %get-tuple-element.13.refs_0_) | copy-start | bytes 786436
  30.3 66.2 %all-to-all-start = ((bf16[192,16,256]{2,1,0:T(8,128)(2,1)}), bf16[192,16,256]{2,1,0:T(8,128)(2,1)S(1)}, u32[]{:S(2)}, u32[]{:S(2)}) async-start(bf16[192,16,256]{2,1,0:T(8,128)(2,1)} %get-tuple-element.12), calls=%async_computation | async-start | bytes 3145728 | tf_op jit(solution)/shard_map/all_to_all | solution.py:332
  43.4 0.7 copy-start.2
  44.1 1.6 %copy-start = (bf16[1024,1024]{1,0:T(8,128)(2,1)S(1)}, bf16[1024,1024]{1,0:T(8,128)(2,1)}, u32[]{:S(2)}) copy-start(bf16[1024,1024]{1,0:T(8,128)(2,1)} %refs_8_.1) | copy-start | bytes 6291460
  45.7 0.9 copy-start.3
  50.0 18.6 %collective-permute-start.9 = (bf16[4,256,128]{2,1,0:T(8,128)(2,1)S(1)}, bf16[4,256,128]{2,1,0:T(8,128)(2,1)S(1)}, u32[]{:S(2)}, u32[]{:S(2)}) collective-permute-start(bf16[4,256,128]{2,1,0:T(8,128)(2,1)S(1)} %get-tuple-element.18), channel_id=1, source_target_pairs={{0,1},{1,2},{2,3},{3,4},{4,5},{5,6},{6,7},{7,0},{8,9},{9,10},{10,1... | collective-permute-start | bytes 786440 | tf_op jit(solution)/shard_map/ppermute | solution.py:287
  54.7 26.2 %collective-permute-start.13 = (bf16[2,256,128]{2,1,0:T(8,128)(2,1)S(1)}, bf16[2,256,128]{2,1,0:T(8,128)(2,1)S(1)}, u32[]{:S(2)}, u32[]{:S(2)}) collective-permute-start(bf16[2,256,128]{2,1,0:T(8,128)(2,1)S(1)} %get-tuple-element.22), channel_id=1, source_target_pairs={{0,6},{1,7},{2,0},{3,1},{4,2},{5,3},{6,4},{7,5},{8,14},{9,15},{10,... | collective-permute-start | bytes 393224 | tf_op jit(solution)/shard_map/ppermute | solution.py:287
  56.6 13.9 %collective-permute-start.10 = (bf16[2,256,128]{2,1,0:T(8,128)(2,1)S(1)}, bf16[2,256,128]{2,1,0:T(8,128)(2,1)S(1)}, u32[]{:S(2)}, u32[]{:S(2)}) collective-permute-start(bf16[2,256,128]{2,1,0:T(8,128)(2,1)S(1)} %get-tuple-element.23), channel_id=1, source_target_pairs={{0,2},{1,3},{2,4},{3,5},{4,6},{5,7},{6,0},{7,1},{8,10},{9,11},{10,... | collective-permute-start | bytes 393224 | tf_op jit(solution)/shard_map/ppermute | solution.py:287
  62.7 20.5 %collective-permute-start.7 = (bf16[4,256,128]{2,1,0:T(8,128)(2,1)S(1)}, bf16[4,256,128]{2,1,0:T(8,128)(2,1)S(1)}, u32[]{:S(2)}, u32[]{:S(2)}) collective-permute-start(bf16[4,256,128]{2,1,0:T(8,128)(2,1)S(1)} %get-tuple-element.15), channel_id=1, source_target_pairs={{0,1},{1,2},{2,3},{3,4},{4,5},{5,6},{6,7},{7,0},{8,9},{9,10},{10,1... | collective-permute-start | bytes 786440 | tf_op jit(solution)/shard_map/ppermute | solution.py:287
  64.6 18.6 %collective-permute-start.8 = (bf16[4,256,128]{2,1,0:T(8,128)(2,1)S(1)}, bf16[4,256,128]{2,1,0:T(8,128)(2,1)S(1)}, u32[]{:S(2)}, u32[]{:S(2)}) collective-permute-start(bf16[4,256,128]{2,1,0:T(8,128)(2,1)S(1)} %get-tuple-element.16), channel_id=1, source_target_pairs={{0,7},{1,0},{2,1},{3,2},{4,3},{5,4},{6,5},{7,6},{8,15},{9,8},{10,9... | collective-permute-start | bytes 786440 | tf_op jit(solution)/shard_map/ppermute | solution.py:287
  68.5 12.3 %collective-permute-start.12 = (bf16[4,256,128]{2,1,0:T(8,128)(2,1)S(1)}, bf16[4,256,128]{2,1,0:T(8,128)(2,1)S(1)}, u32[]{:S(2)}, u32[]{:S(2)}) collective-permute-start(bf16[4,256,128]{2,1,0:T(8,128)(2,1)S(1)} %get-tuple-element.21), channel_id=1, source_target_pairs={{0,7},{1,0},{2,1},{3,2},{4,3},{5,4},{6,5},{7,6},{8,15},{9,8},{10,9... | collective-permute-start | bytes 786440 | tf_op jit(solution)/shard_map/ppermute | solution.py:287
  70.7 15.2 %collective-permute-start.11 = (bf16[4,256,128]{2,1,0:T(8,128)(2,1)S(1)}, bf16[4,256,128]{2,1,0:T(8,128)(2,1)S(1)}, u32[]{:S(2)}, u32[]{:S(2)}) collective-permute-start(bf16[4,256,128]{2,1,0:T(8,128)(2,1)S(1)} %pad_maximum_fusion), channel_id=1, source_target_pairs={{0,2},{1,3},{2,4},{3,5},{4,6},{5,7},{6,0},{7,1},{8,10},{9,11},{10,... | collective-permute-start | bytes 786440 | tf_op jit(solution)/shard_map/ppermute | solution.py:287
  81.0 15.5 %collective-permute-start.14 = (bf16[4,256,128]{2,1,0:T(8,128)(2,1)S(1)}, bf16[4,256,128]{2,1,0:T(8,128)(2,1)S(1)}, u32[]{:S(2)}, u32[]{:S(2)}) collective-permute-start(bf16[4,256,128]{2,1,0:T(8,128)(2,1)S(1)} %pad_maximum_fusion.1), channel_id=1, source_target_pairs={{0,6},{1,7},{2,0},{3,1},{4,2},{5,3},{6,4},{7,5},{8,14},{9,15},{10,... | collective-permute-start | bytes 786440 | tf_op jit(solution)/shard_map/ppermute | solution.py:287

commit v3 on v2

--- a/solution.py
+++ b/solution.py
@@ -244,40 +244,35 @@
     return parts, jnp.stack(place)
 
 
-def finish_kernel(migrated_hbm, *refs):
-    terms, (out, moved_hbm, moved) = refs[:-3], refs[-3:]
-    copy = pltpu.make_async_copy(migrated_hbm, moved_hbm, moved)
-    copy.start()
-    out[...] = sum(term[...].astype(jnp.float32) for term in terms).astype(out.dtype)
-    copy.wait()
-
-
-def finish(migrated, terms):
+def move_kernel(source, target, held, arrived, left):
+    parts = arrived.shape[0]
+    rows = held.shape[0] // parts
+    spans = [pl.ds(i * rows, rows) for i in range(parts)]
+    loads = start_all([(source.at[span], held.at[span]) for span in spans], arrived)
+    stores = []
+    for i, span in enumerate(spans):
+        loads[i].wait()
+        stores += start_all([(held.at[span], target.at[span])], left.at[pl.ds(i, 1)])
+    for store in stores:
+        store.wait()
+
+
+def move(migrated):
     far = pl.BlockSpec(memory_space=pltpu.HBM)
-    vmem = pl.BlockSpec(memory_space=pltpu.VMEM)
     return pl.pallas_call(
-        finish_kernel,
-        out_shape=[
-            jax.ShapeDtypeStruct(terms[0].shape, jnp.bfloat16),
-            jax.ShapeDtypeStruct(migrated.shape, migrated.dtype),
+        move_kernel,
+        out_shape=jax.ShapeDtypeStruct(migrated.shape, migrated.dtype),
+        in_specs=[far],
+        out_specs=far,
+        scratch_shapes=[
+            pltpu.VMEM(migrated.shape, migrated.dtype),
+            pltpu.SemaphoreType.DMA((4,)),
+            pltpu.SemaphoreType.DMA((4,)),
         ],
-        in_specs=[far] + [vmem] * len(terms),
-        out_specs=[vmem, far],
-        scratch_shapes=[pltpu.SemaphoreType.DMA],
-        compiler_params=pltpu.CompilerParams(vmem_limit_bytes=32 << 20),
-        cost_estimate=pl.CostEstimate(flops=0, bytes_accessed=4 << 20, transcendentals=0),
-        name="finish",
-    )(migrated, *terms)
-
-
-def signs(me):
-    return 1 - 2 * (me % 2), 1 - 2 * (me // 2 % 2)
-
-
-def share_order(me):
-    near, next_near = signs(me)
-    offsets = (4, 3 * near, -3 * near, 2 * next_near, -2 * next_near, near, -near, 0)
-    return jnp.stack([(me + offset) % SHARES for offset in offsets])
+        compiler_params=pltpu.CompilerParams(vmem_limit_bytes=60 << 20),
+        cost_estimate=pl.CostEstimate(flops=0, bytes_accessed=3 << 20, transcendentals=0),
+        name="move",
+    )(migrated)
 
 
 def send_round_ring(blocks):
@@ -292,8 +287,8 @@
     half = blocks[4].shape[0] // 2
     far_up = shift(blocks[4][:half], 2)
     far_down = shift(blocks[4][half:], -2)
-    up, down = shift(blocks[3], 1), shift(blocks[-3], -1)
-    near_up, near_down = shift(blocks[1], 1), shift(blocks[-1], -1)
+    up, near_up = shift(jnp.stack([blocks[3], blocks[1]]), 1)
+    down, near_down = shift(jnp.stack([blocks[-3], blocks[-1]]), -1)
     above = total(blocks[2], up)
     above = jnp.concatenate([above[:half] + far_up.astype(jnp.float32), above[half:]], 0)
     below = total(blocks[-2], down)
@@ -332,7 +327,10 @@
     migrated = lax.all_to_all(packed, ("grp", "seq"), split_axis=0, concat_axis=0, tiled=True)
     me = lax.axis_index("tp").reshape(1)
     terms = send_round_ring(dict(zip(OFFSETS, project(me, place, parts, out_proj))))
-    decoded, migrated = finish(migrated, terms)
+    migrated = move(migrated)
+    migrated, own = lax.optimization_barrier((migrated, terms[0]))
+    terms = (own,) + terms[1:]
+    decoded = sum(term.astype(jnp.float32) for term in terms).astype(jnp.bfloat16)
     return (decoded, migrated)
 
 

time: 99.1 us -> 95.5 us (0.964)
  the two profiles are of different devices: /device:TPU:26 before, /device:TPU:4 now
where the time goes in v3:
time: 95.5 us; the launch traced here: 94.8 us
  starting transfers between devices  61.1 us (64%)
  waiting for transfers between devices  18.9 us (20%)
  Pallas kernels  10.8 us (11%)
  local copies, waits for them, and re-layouts  1.8 us (2%)
  other arithmetic  1.2 us (1%)
  between operations  1 us (1%)
    ppermute x6, starting transfers between devices, shift(): lax.ppermute(block, 'tp', [(i, (i + by) % size) for i in range(size)])  23.7 us
    ppermute x6, starting transfers between devices, shift(): return lax.ppermute(block, 'seq', pairs)  19.1 us
    ppermute x6, waiting for transfers between devices, shift(): lax.ppermute(block, 'tp', [(i, (i + by) % size) for i in range(size)])  16.1 us
    all_to_all x1, starting transfers between devices, per_device(): lax.all_to_all(packed, ('grp', 'seq'), split_axis=0, concat_axis=0, tiled...  14.1 us
    pallas_call x1, Pallas kernels, attend_and_pack(): pl.pallas_call(attend_kernel, out_shape=[jax.ShapeDtypeStruct(queries.sha...  5.09 us
    ppermute x1, starting transfers between devices, gather_heads(): lax.ppermute(heads, 'seq', [(i, (i + along) % (2 * along)) for i in range...  4.28 us
    pallas_call x1, Pallas kernels, project(): pl.pallas_call(project_kernel, out_shape=[block] * len(OFFSETS), in_specs...  3.52 us
    all_to_all x1, waiting for transfers between devices, per_device(): lax.all_to_all(packed, ('grp', 'seq'), split_axis=0, concat_axis=0, tiled...  2.75 us
  transfers between devices with their start and end apart: 14, of which 6 were waited for; matrix products, arithmetic and copies ran while one was open for 0% of the time, Pallas kernels for 6%

profile of v3, /device:TPU:4, one launch (start us, length us, event | category | flops | bytes accessed | tf_op | source)
XLA Modules:
  0.0 94.8 jit_solution(6389958191330552660)
XLA Ops:
  0.6 5.1 %attend_and_pack.1 = (bf16[4,32,1024]{2,1,0:T(8,128)(2,1)}, bf16[192,16,256]{2,1,0:T(8,128)(2,1)}) custom-call(s32[1,32]{1,0:T(1,128)} %blocks_hbm.1, s32[1,32]{1,0:T(1,128)} %tail_hbm.1, s32[1,32]{1,0:T(1,128)} %owner_hbm.1, bf16[64,16,256]{2,1,0:T(8,128)(2,1)} %finished_hbm.1, s32[2,32]{1,0:T(2,128)} %bitcast.38, s32[1,32]{1,0:T(1,128)} %length_hbm.1, ...), custom_call_target="tpu_custom_call" | custom-call | flops 301989888 | bytes 5242880 | tf_op jit(solution)/shard_map/attend_and_pack/pallas_call | solution.py:153
  5.7 4.3 %collective-permute-start = (bf16[4,32,1024]{2,1,0:T(8,128)(2,1)}, bf16[4,32,1024]{2,1,0:T(8,128)(2,1)S(1)}, u32[]{:S(2)}, u32[]{:S(2)}) collective-permute-start(bf16[4,32,1024]{2,1,0:T(8,128)(2,1)} %get-tuple-element.15.refs_0_), channel_id=1, source_target_pairs={{0,32},{8,40},{16,48},{24,56},{32,0},{40,8},{48,16},{56,24},{1,33}... | collective-permute-start | bytes 786440 | tf_op jit(solution)/shard_map/ppermute | solution.py:238
  10.0 5.4 %collective-permute-start.3 = (bf16[4,32,1024]{2,1,0:T(8,128)(2,1)}, bf16[4,32,1024]{2,1,0:T(8,128)(2,1)S(1)}, u32[]{:S(2)}, u32[]{:S(2)}) collective-permute-start(bf16[4,32,1024]{2,1,0:T(8,128)(2,1)} %get-tuple-element.15.refs_0_), channel_id=1, source_target_pairs={{0,16},{8,24},{16,0},{24,8},{32,48},{40,56},{48,32},{56,40},{1,17}... | collective-permute-start | bytes 786440 | tf_op jit(solution)/shard_map/ppermute | solution.py:234
  15.5 1.9 %collective-permute-start.2 = (bf16[4,32,1024]{2,1,0:T(8,128)(2,1)}, bf16[4,32,1024]{2,1,0:T(8,128)(2,1)S(1)}, u32[]{:S(2)}, u32[]{:S(2)}) collective-permute-start(bf16[4,32,1024]{2,1,0:T(8,128)(2,1)} %get-tuple-element.15.refs_0_), channel_id=1, source_target_pairs={{0,24},{8,0},{16,8},{24,16},{32,56},{40,32},{48,40},{56,48},{1,25}... | collective-permute-start | bytes 786440 | tf_op jit(solution)/shard_map/ppermute | solution.py:234
  17.4 3.9 %collective-permute-start.1 = (bf16[4,32,1024]{2,1,0:T(8,128)(2,1)}, bf16[4,32,1024]{2,1,0:T(8,128)(2,1)S(1)}, u32[]{:S(2)}, u32[]{:S(2)}) collective-permute-start(bf16[4,32,1024]{2,1,0:T(8,128)(2,1)} %get-tuple-element.15.refs_0_), channel_id=1, source_target_pairs={{0,8},{8,16},{16,24},{24,0},{32,40},{40,48},{48,56},{56,32},{1,9},... | collective-permute-start | bytes 786440 | tf_op jit(solution)/shard_map/ppermute | solution.py:234
  21.3 0.0 collective-permute-done.refs_1_
  21.3 1.9 %collective-permute-start.6 = (bf16[4,32,1024]{2,1,0:T(8,128)(2,1)S(1)}, bf16[4,32,1024]{2,1,0:T(8,128)(2,1)}, u32[]{:S(2)}, u32[]{:S(2)}) collective-permute-start(bf16[4,32,1024]{2,1,0:T(8,128)(2,1)S(1)} %collective-permute-done.refs_1_), channel_id=1, source_target_pairs={{0,16},{8,24},{16,0},{24,8},{32,48},{40,56},{48,32},{56,40},{1,17}... | collective-permute-start | bytes 786440 | tf_op jit(solution)/shard_map/ppermute | solution.py:234
  23.3 3.7 %collective-permute-start.5 = (bf16[4,32,1024]{2,1,0:T(8,128)(2,1)S(1)}, bf16[4,32,1024]{2,1,0:T(8,128)(2,1)}, u32[]{:S(2)}, u32[]{:S(2)}) collective-permute-start(bf16[4,32,1024]{2,1,0:T(8,128)(2,1)S(1)} %collective-permute-done.refs_1_), channel_id=1, source_target_pairs={{0,24},{8,0},{16,8},{24,16},{32,56},{40,32},{48,40},{56,48},{1,25}... | collective-permute-start | bytes 786440 | tf_op jit(solution)/shard_map/ppermute | solution.py:234
  26.9 0.0 collective-permute-done.3.refs_4_
  26.9 2.2 %collective-permute-start.4 = (bf16[4,32,1024]{2,1,0:T(8,128)(2,1)S(1)}, bf16[4,32,1024]{2,1,0:T(8,128)(2,1)}, u32[]{:S(2)}, u32[]{:S(2)}) collective-permute-start(bf16[4,32,1024]{2,1,0:T(8,128)(2,1)S(1)} %collective-permute-done.refs_1_), channel_id=1, source_target_pairs={{0,8},{8,16},{16,24},{24,0},{32,40},{40,48},{48,56},{56,32},{1,9},... | collective-permute-start | bytes 786440 | tf_op jit(solution)/shard_map/ppermute | solution.py:234
  29.2 0.0 copy-start
  29.2 0.0 copy-start.1
  29.2 14.1 %all-to-all-start = ((bf16[192,16,256]{2,1,0:T(8,128)(2,1)}), bf16[192,16,256]{2,1,0:T(8,128)(2,1)}, u32[]{:S(2)}, u32[]{:S(2)}) async-start(bf16[192,16,256]{2,1,0:T(8,128)(2,1)} %get-tuple-element.14), calls=%async_computation | async-start | bytes 3145728 | tf_op jit(solution)/shard_map/all_to_all | solution.py:327
  43.4 0.1 stack.53.place
  43.5 0.0 collective-permute-done.2.refs_3_
  43.5 0.0 collective-permute-done.1.refs_2_
  43.5 0.0 copy-start.2
  43.5 0.7 copy-done.2
  44.2 0.0 collective-permute-done.6.refs_7_
  44.2 0.0 collective-permute-done.5.refs_6_
  44.2 0.0 collective-permute-done.4.refs_5_
  44.2 0.0 copy-done
  44.2 0.0 copy-done.1
  44.2 0.0 copy-start.3
  44.3 0.9 copy-done.3
  45.2 3.5 %project.1 = (bf16[4,256,128]{2,1,0:T(8,128)(2,1)S(1)}, bf16[4,256,128]{2,1,0:T(8,128)(2,1)S(1)}, bf16[4,256,128]{2,1,0:T(8,128)(2,1)S(1)}, bf16[4,256,128]{2,1,...) custom-call(s32[1]{0:T(128)} %bitcast.1.me, ...), custom_call_target="tpu_custom_call" | custom-call | flops 21474836480 | bytes 6291456 | tf_op jit(solution)/shard_map/project/pallas_call | solution.py:214
  48.7 0.1 pad_maximum_fusion.1
  48.8 5.4 %collective-permute-start.8 = (bf16[2,4,256,128]{3,2,1,0:T(8,128)(2,1)S(1)}, bf16[2,4,256,128]{3,2,1,0:T(8,128)(2,1)S(1)}, u32[]{:S(2)}, u32[]{:S(2)}) collective-permute-start(bf16[2,4,256,128]{3,2,1,0:T(8,128)(2,1)S(1)} %pad_maximum_fusion.1), channel_id=1, source_target_pairs={{0,7},{1,0},{2,1},{3,2},{4,3},{5,4},{6,5},{7,6},{8,15},{9,8},{10,9... | collective-permute-start | bytes 1572872 | tf_op jit(solution)/shard_map/ppermute | solution.py:282
  54.2 1.9 %collective-permute-start.9 = (bf16[2,256,128]{2,1,0:T(8,128)(2,1)S(1)}, bf16[2,256,128]{2,1,0:T(8,128)(2,1)S(1)}, u32[]{:S(2)}, u32[]{:S(2)}) collective-permute-start(bf16[2,256,128]{2,1,0:T(8,128)(2,1)S(1)} %get-tuple-element.26), channel_id=1, source_target_pairs={{0,2},{1,3},{2,4},{3,5},{4,6},{5,7},{6,0},{7,1},{8,10},{9,11},{10,... | collective-permute-start | bytes 393224 | tf_op jit(solution)/shard_map/ppermute | solution.py:282
  56.1 6.0 %collective-permute-start.11 = (bf16[2,256,128]{2,1,0:T(8,128)(2,1)S(1)}, bf16[2,256,128]{2,1,0:T(8,128)(2,1)S(1)}, u32[]{:S(2)}, u32[]{:S(2)}) collective-permute-start(bf16[2,256,128]{2,1,0:T(8,128)(2,1)S(1)} %get-tuple-element.27), channel_id=1, source_target_pairs={{0,6},{1,7},{2,0},{3,1},{4,2},{5,3},{6,4},{7,5},{8,14},{9,15},{10,... | collective-permute-start | bytes 393224 | tf_op jit(solution)/shard_map/ppermute | solution.py:282
  62.2 0.1 pad_maximum_fusion
  62.2 1.9 %collective-permute-start.7 = (bf16[2,4,256,128]{3,2,1,0:T(8,128)(2,1)S(1)}, bf16[2,4,256,128]{3,2,1,0:T(8,128)(2,1)S(1)}, u32[]{:S(2)}, u32[]{:S(2)}) collective-permute-start(bf16[2,4,256,128]{3,2,1,0:T(8,128)(2,1)S(1)} %pad_maximum_fusion), channel_id=1, source_target_pairs={{0,1},{1,2},{2,3},{3,4},{4,5},{5,6},{6,7},{7,0},{8,9},{9,10},{10,1... | collective-permute-start | bytes 1572872 | tf_op jit(solution)/shard_map/ppermute | solution.py:282
  64.2 5.1 %collective-permute-done.8 = bf16[2,4,256,128]{3,2,1,0:T(8,128)(2,1)S(1)} collective-permute-done((bf16[2,4,256,128]{3,2,1,0:T(8,128)(2,1)S(1)}, bf16[2,4,256,128]{3,2,1,0:T(8,128)(2,1)S(1)}, u32[]{:S(2)}, u32[]{:S(2)}) %collective-permute-start.8) | collective-permute-done | bytes 524320 | tf_op jit(solution)/shard_map/ppermute | solution.py:282
  69.2 0.1 convert_add_fusion
  69.3 1.9 %collective-permute-done.11 = bf16[2,256,128]{2,1,0:T(8,128)(2,1)S(1)} collective-permute-done((bf16[2,256,128]{2,1,0:T(8,128)(2,1)S(1)}, bf16[2,256,128]{2,1,0:T(8,128)(2,1)S(1)}, u32[]{:S(2)}, u32[]{:S(2)}) %collective-permute-start.11) | collective-permute-done | bytes 131104 | tf_op jit(solution)/shard_map/ppermute | solution.py:282
  71.3 6.5 %collective-permute-start.12 = (bf16[4,256,128]{2,1,0:T(8,128)(2,1)S(1)}, bf16[4,256,128]{2,1,0:T(8,128)(2,1)S(1)}, u32[]{:S(2)}, u32[]{:S(2)}) collective-permute-start(bf16[4,256,128]{2,1,0:T(8,128)(2,1)S(1)} %pad_maximum_fusion.3), channel_id=1, source_target_pairs={{0,6},{1,7},{2,0},{3,1},{4,2},{5,3},{6,4},{7,5},{8,14},{9,15},{10,... | collective-permute-start | bytes 786440 | tf_op jit(solution)/shard_map/ppermute | solution.py:282
  77.8 0.6 collective-permute-done.7
  78.5 0.1 convert_add_fusion.1
  78.6 0.0 collective-permute-done.9
  78.6 1.9 %collective-permute-start.10 = (bf16[4,256,128]{2,1,0:T(8,128)(2,1)S(1)}, bf16[4,256,128]{2,1,0:T(8,128)(2,1)S(1)}, u32[]{:S(2)}, u32[]{:S(2)}) collective-permute-start(bf16[4,256,128]{2,1,0:T(8,128)(2,1)S(1)} %pad_maximum_fusion.2), channel_id=1, source_target_pairs={{0,2},{1,3},{2,4},{3,5},{4,6},{5,7},{6,0},{7,1},{8,10},{9,11},{10,... | collective-permute-start | bytes 786440 | tf_op jit(solution)/shard_map/ppermute | solution.py:282
  80.6 2.8 %all-to-all-done.source = bf16[192,16,256]{2,1,0:T(8,128)(2,1)} async-done(((bf16[192,16,256]{2,1,0:T(8,128)(2,1)}), bf16[192,16,256]{2,1,0:T(8,128)(2,1)}, u32[]{:S(2)}, u32[]{:S(2)}) %all-to-all-start) | async-done | bytes 1572896 | tf_op jit(solution)/shard_map/all_to_all | solution.py:327
  83.3 2.2 %move.1 = bf16[192,16,256]{2,1,0:T(8,128)(2,1)} custom-call(bf16[192,16,256]{2,1,0:T(8,128)(2,1)} %all-to-all-done.source), custom_call_target="tpu_custom_call" | custom-call | bytes 3145728 | tf_op jit(solution)/shard_map/move/pallas_call | solution.py:262
  85.5 1.8 %collective-permute-done.12 = bf16[4,256,128]{2,1,0:T(8,128)(2,1)S(1)} collective-permute-done((bf16[4,256,128]{2,1,0:T(8,128)(2,1)S(1)}, bf16[4,256,128]{2,1,0:T(8,128)(2,1)S(1)}, u32[]{:S(2)}, u32[]{:S(2)}) %collective-permute-start.12) | collective-permute-done | bytes 262176 | tf_op jit(solution)/shard_map/ppermute | solution.py:282
  87.3 6.6 %collective-permute-done.10 = bf16[4,256,128]{2,1,0:T(8,128)(2,1)S(1)} collective-permute-done((bf16[4,256,128]{2,1,0:T(8,128)(2,1)S(1)}, bf16[4,256,128]{2,1,0:T(8,128)(2,1)S(1)}, u32[]{:S(2)}, u32[]{:S(2)}) %collective-permute-start.10) | collective-permute-done | bytes 262176 | tf_op jit(solution)/shard_map/ppermute | solution.py:282
  93.9 0.9 fusion.2
  (7 shorter events, 0.2 us)
Async XLA Ops:
  5.7 15.6 %collective-permute-start = (bf16[4,32,1024]{2,1,0:T(8,128)(2,1)}, bf16[4,32,1024]{2,1,0:T(8,128)(2,1)S(1)}, u32[]{:S(2)}, u32[]{:S(2)}) collective-permute-start(bf16[4,32,1024]{2,1,0:T(8,128)(2,1)} %get-tuple-element.15.refs_0_), channel_id=1, source_target_pairs={{0,32},{8,40},{16,48},{24,56},{32,0},{40,8},{48,16},{56,24},{1,33}... | collective-permute-start | bytes 786440 | tf_op jit(solution)/shard_map/ppermute | solution.py:238
  10.0 16.9 %collective-permute-start.3 = (bf16[4,32,1024]{2,1,0:T(8,128)(2,1)}, bf16[4,32,1024]{2,1,0:T(8,128)(2,1)S(1)}, u32[]{:S(2)}, u32[]{:S(2)}) collective-permute-start(bf16[4,32,1024]{2,1,0:T(8,128)(2,1)} %get-tuple-element.15.refs_0_), channel_id=1, source_target_pairs={{0,16},{8,24},{16,0},{24,8},{32,48},{40,56},{48,32},{56,40},{1,17}... | collective-permute-start | bytes 786440 | tf_op jit(solution)/shard_map/ppermute | solution.py:234
  15.5 28.0 %collective-permute-start.2 = (bf16[4,32,1024]{2,1,0:T(8,128)(2,1)}, bf16[4,32,1024]{2,1,0:T(8,128)(2,1)S(1)}, u32[]{:S(2)}, u32[]{:S(2)}) collective-permute-start(bf16[4,32,1024]{2,1,0:T(8,128)(2,1)} %get-tuple-element.15.refs_0_), channel_id=1, source_target_pairs={{0,24},{8,0},{16,8},{24,16},{32,56},{40,32},{48,40},{56,48},{1,25}... | collective-permute-start | bytes 786440 | tf_op jit(solution)/shard_map/ppermute | solution.py:234
  17.4 26.1 %collective-permute-start.1 = (bf16[4,32,1024]{2,1,0:T(8,128)(2,1)}, bf16[4,32,1024]{2,1,0:T(8,128)(2,1)S(1)}, u32[]{:S(2)}, u32[]{:S(2)}) collective-permute-start(bf16[4,32,1024]{2,1,0:T(8,128)(2,1)} %get-tuple-element.15.refs_0_), channel_id=1, source_target_pairs={{0,8},{8,16},{16,24},{24,0},{32,40},{40,48},{48,56},{56,32},{1,9},... | collective-permute-start | bytes 786440 | tf_op jit(solution)/shard_map/ppermute | solution.py:234
  21.3 22.9 %collective-permute-start.6 = (bf16[4,32,1024]{2,1,0:T(8,128)(2,1)S(1)}, bf16[4,32,1024]{2,1,0:T(8,128)(2,1)}, u32[]{:S(2)}, u32[]{:S(2)}) collective-permute-start(bf16[4,32,1024]{2,1,0:T(8,128)(2,1)S(1)} %collective-permute-done.refs_1_), channel_id=1, source_target_pairs={{0,16},{8,24},{16,0},{24,8},{32,48},{40,56},{48,32},{56,40},{1,17}... | collective-permute-start | bytes 786440 | tf_op jit(solution)/shard_map/ppermute | solution.py:234
  23.3 21.0 %collective-permute-start.5 = (bf16[4,32,1024]{2,1,0:T(8,128)(2,1)S(1)}, bf16[4,32,1024]{2,1,0:T(8,128)(2,1)}, u32[]{:S(2)}, u32[]{:S(2)}) collective-permute-start(bf16[4,32,1024]{2,1,0:T(8,128)(2,1)S(1)} %collective-permute-done.refs_1_), channel_id=1, source_target_pairs={{0,24},{8,0},{16,8},{24,16},{32,56},{40,32},{48,40},{56,48},{1,25}... | collective-permute-start | bytes 786440 | tf_op jit(solution)/shard_map/ppermute | solution.py:234
  26.9 17.3 %collective-permute-start.4 = (bf16[4,32,1024]{2,1,0:T(8,128)(2,1)S(1)}, bf16[4,32,1024]{2,1,0:T(8,128)(2,1)}, u32[]{:S(2)}, u32[]{:S(2)}) collective-permute-start(bf16[4,32,1024]{2,1,0:T(8,128)(2,1)S(1)} %collective-permute-done.refs_1_), channel_id=1, source_target_pairs={{0,8},{8,16},{16,24},{24,0},{32,40},{40,48},{48,56},{56,32},{1,9},... | collective-permute-start | bytes 786440 | tf_op jit(solution)/shard_map/ppermute | solution.py:234
  29.2 15.0 %copy-start = (bf16[1024,1024]{1,0:T(8,128)(2,1)S(1)}, bf16[1024,1024]{1,0:T(8,128)(2,1)}, u32[]{:S(2)}) copy-start(bf16[1024,1024]{1,0:T(8,128)(2,1)} %refs_8_.1) | copy-start | bytes 6291460
  29.2 15.0 %copy-start.1 = (bf16[4,32,1024]{2,1,0:T(8,128)(2,1)S(1)}, bf16[4,32,1024]{2,1,0:T(8,128)(2,1)}, u32[]{:S(2)}) copy-start(bf16[4,32,1024]{2,1,0:T(8,128)(2,1)} %get-tuple-element.15.refs_0_) | copy-start | bytes 786436
  29.2 54.1 %all-to-all-start = ((bf16[192,16,256]{2,1,0:T(8,128)(2,1)}), bf16[192,16,256]{2,1,0:T(8,128)(2,1)}, u32[]{:S(2)}, u32[]{:S(2)}) async-start(bf16[192,16,256]{2,1,0:T(8,128)(2,1)} %get-tuple-element.14), calls=%async_computation | async-start | bytes 3145728 | tf_op jit(solution)/shard_map/all_to_all | solution.py:327
  43.5 0.7 copy-start.2
  44.2 1.0 %copy-start.3 = (bf16[4,32,1024]{2,1,0:T(8,128)(2,1)S(1)}, bf16[4,32,1024]{2,1,0:T(8,128)(2,1)}, u32[]{:S(2)}) copy-start(bf16[4,32,1024]{2,1,0:T(8,128)(2,1)} %copy-done.2) | copy-start | bytes 786436
  48.8 20.5 %collective-permute-start.8 = (bf16[2,4,256,128]{3,2,1,0:T(8,128)(2,1)S(1)}, bf16[2,4,256,128]{3,2,1,0:T(8,128)(2,1)S(1)}, u32[]{:S(2)}, u32[]{:S(2)}) collective-permute-start(bf16[2,4,256,128]{3,2,1,0:T(8,128)(2,1)S(1)} %pad_maximum_fusion.1), channel_id=1, source_target_pairs={{0,7},{1,0},{2,1},{3,2},{4,3},{5,4},{6,5},{7,6},{8,15},{9,8},{10,9... | collective-permute-start | bytes 1572872 | tf_op jit(solution)/shard_map/ppermute | solution.py:282
  54.2 24.4 %collective-permute-start.9 = (bf16[2,256,128]{2,1,0:T(8,128)(2,1)S(1)}, bf16[2,256,128]{2,1,0:T(8,128)(2,1)S(1)}, u32[]{:S(2)}, u32[]{:S(2)}) collective-permute-start(bf16[2,256,128]{2,1,0:T(8,128)(2,1)S(1)} %get-tuple-element.26), channel_id=1, source_target_pairs={{0,2},{1,3},{2,4},{3,5},{4,6},{5,7},{6,0},{7,1},{8,10},{9,11},{10,... | collective-permute-start | bytes 393224 | tf_op jit(solution)/shard_map/ppermute | solution.py:282
  56.1 15.2 %collective-permute-start.11 = (bf16[2,256,128]{2,1,0:T(8,128)(2,1)S(1)}, bf16[2,256,128]{2,1,0:T(8,128)(2,1)S(1)}, u32[]{:S(2)}, u32[]{:S(2)}) collective-permute-start(bf16[2,256,128]{2,1,0:T(8,128)(2,1)S(1)} %get-tuple-element.27), channel_id=1, source_target_pairs={{0,6},{1,7},{2,0},{3,1},{4,2},{5,3},{6,4},{7,5},{8,14},{9,15},{10,... | collective-permute-start | bytes 393224 | tf_op jit(solution)/shard_map/ppermute | solution.py:282
  62.2 16.2 %collective-permute-start.7 = (bf16[2,4,256,128]{3,2,1,0:T(8,128)(2,1)S(1)}, bf16[2,4,256,128]{3,2,1,0:T(8,128)(2,1)S(1)}, u32[]{:S(2)}, u32[]{:S(2)}) collective-permute-start(bf16[2,4,256,128]{3,2,1,0:T(8,128)(2,1)S(1)} %pad_maximum_fusion), channel_id=1, source_target_pairs={{0,1},{1,2},{2,3},{3,4},{4,5},{5,6},{6,7},{7,0},{8,9},{9,10},{10,1... | collective-permute-start | bytes 1572872 | tf_op jit(solution)/shard_map/ppermute | solution.py:282
  71.3 16.0 %collective-permute-start.12 = (bf16[4,256,128]{2,1,0:T(8,128)(2,1)S(1)}, bf16[4,256,128]{2,1,0:T(8,128)(2,1)S(1)}, u32[]{:S(2)}, u32[]{:S(2)}) collective-permute-start(bf16[4,256,128]{2,1,0:T(8,128)(2,1)S(1)} %pad_maximum_fusion.3), channel_id=1, source_target_pairs={{0,6},{1,7},{2,0},{3,1},{4,2},{5,3},{6,4},{7,5},{8,14},{9,15},{10,... | collective-permute-start | bytes 786440 | tf_op jit(solution)/shard_map/ppermute | solution.py:282
  78.6 15.3 %collective-permute-start.10 = (bf16[4,256,128]{2,1,0:T(8,128)(2,1)S(1)}, bf16[4,256,128]{2,1,0:T(8,128)(2,1)S(1)}, u32[]{:S(2)}, u32[]{:S(2)}) collective-permute-start(bf16[4,256,128]{2,1,0:T(8,128)(2,1)S(1)} %pad_maximum_fusion.2), channel_id=1, source_target_pairs={{0,2},{1,3},{2,4},{3,5},{4,6},{5,7},{6,0},{7,1},{8,10},{9,11},{10,... | collective-permute-start | bytes 786440 | tf_op jit(solution)/shard_map/ppermute | solution.py:282

commit v4 on v3

--- a/solution.py
+++ b/solution.py
@@ -91,10 +91,12 @@
         for s in range(steps)
     ]
     tile_row = index(cached, 0)
-    for load in loads:
+    for load in loads[:4]:
         load.wait()
     pack_blocks(blocks, tail, owner, finished, packed)
     (store,) = start_all([(packed, packed_hbm)], left)
+    for load in loads[4:]:
+        load.wait()
     groups = range(rows // GROUP)
     cached_bias = []
     for g in groups:

time: 95.5 us -> 94.5 us (0.990)
  Pallas kernels: 10.8 us -> 9.76 us
    pallas_call x1, Pallas kernels: 5.09 us -> 4.05 us  [attend_and_pack(): pl.pallas_call(attend_kernel, out_shape=[jax.ShapeDtypeStruct(queries.sha...]
where the time goes in v4:
time: 94.5 us; the launch traced here: 93.8 us
  starting transfers between devices  61.1 us (65%)
  waiting for transfers between devices  18.9 us (20%)
  Pallas kernels  9.76 us (10%)
  local copies, waits for them, and re-layouts  1.8 us (2%)
  other arithmetic  1.2 us (1%)
  between operations  1 us (1%)
    ppermute x6, starting transfers between devices, shift(): lax.ppermute(block, 'tp', [(i, (i + by) % size) for i in range(size)])  23.7 us
    ppermute x6, starting transfers between devices, shift(): return lax.ppermute(block, 'seq', pairs)  19.1 us
    ppermute x6, waiting for transfers between devices, shift(): lax.ppermute(block, 'tp', [(i, (i + by) % size) for i in range(size)])  16.1 us
    all_to_all x1, starting transfers between devices, per_device(): lax.all_to_all(packed, ('grp', 'seq'), split_axis=0, concat_axis=0, tiled...  14.1 us
    ppermute x1, starting transfers between devices, gather_heads(): lax.ppermute(heads, 'seq', [(i, (i + along) % (2 * along)) for i in range...  4.28 us
    pallas_call x1, Pallas kernels, attend_and_pack(): pl.pallas_call(attend_kernel, out_shape=[jax.ShapeDtypeStruct(queries.sha...  4.05 us
    pallas_call x1, Pallas kernels, project(): pl.pallas_call(project_kernel, out_shape=[block] * len(OFFSETS), in_specs...  3.52 us
    all_to_all x1, waiting for transfers between devices, per_device(): lax.all_to_all(packed, ('grp', 'seq'), split_axis=0, concat_axis=0, tiled...  2.75 us
  transfers between devices with their start and end apart: 14, of which 6 were waited for; matrix products, arithmetic and copies ran while one was open for 0% of the time, Pallas kernels for 6%

profile of v4, /device:TPU:4, one launch (start us, length us, event | category | flops | bytes accessed | tf_op | source)
XLA Modules:
  0.0 93.8 jit_solution(17975495714926956094)
XLA Ops:
  0.6 4.1 %attend_and_pack.1 = (bf16[4,32,1024]{2,1,0:T(8,128)(2,1)}, bf16[192,16,256]{2,1,0:T(8,128)(2,1)}) custom-call(s32[1,32]{1,0:T(1,128)} %blocks_hbm.1, s32[1,32]{1,0:T(1,128)} %tail_hbm.1, s32[1,32]{1,0:T(1,128)} %owner_hbm.1, bf16[64,16,256]{2,1,0:T(8,128)(2,1)} %finished_hbm.1, s32[2,32]{1,0:T(2,128)} %bitcast.38, s32[1,32]{1,0:T(1,128)} %length_hbm.1, ...), custom_call_target="tpu_custom_call" | custom-call | flops 301989888 | bytes 5242880 | tf_op jit(solution)/shard_map/attend_and_pack/pallas_call | solution.py:155
  4.7 4.3 %collective-permute-start = (bf16[4,32,1024]{2,1,0:T(8,128)(2,1)}, bf16[4,32,1024]{2,1,0:T(8,128)(2,1)S(1)}, u32[]{:S(2)}, u32[]{:S(2)}) collective-permute-start(bf16[4,32,1024]{2,1,0:T(8,128)(2,1)} %get-tuple-element.15.refs_0_), channel_id=1, source_target_pairs={{0,32},{8,40},{16,48},{24,56},{32,0},{40,8},{48,16},{56,24},{1,33}... | collective-permute-start | bytes 786440 | tf_op jit(solution)/shard_map/ppermute | solution.py:240
  9.0 5.4 %collective-permute-start.3 = (bf16[4,32,1024]{2,1,0:T(8,128)(2,1)}, bf16[4,32,1024]{2,1,0:T(8,128)(2,1)S(1)}, u32[]{:S(2)}, u32[]{:S(2)}) collective-permute-start(bf16[4,32,1024]{2,1,0:T(8,128)(2,1)} %get-tuple-element.15.refs_0_), channel_id=1, source_target_pairs={{0,16},{8,24},{16,0},{24,8},{32,48},{40,56},{48,32},{56,40},{1,17}... | collective-permute-start | bytes 786440 | tf_op jit(solution)/shard_map/ppermute | solution.py:236
  14.4 1.9 %collective-permute-start.2 = (bf16[4,32,1024]{2,1,0:T(8,128)(2,1)}, bf16[4,32,1024]{2,1,0:T(8,128)(2,1)S(1)}, u32[]{:S(2)}, u32[]{:S(2)}) collective-permute-start(bf16[4,32,1024]{2,1,0:T(8,128)(2,1)} %get-tuple-element.15.refs_0_), channel_id=1, source_target_pairs={{0,24},{8,0},{16,8},{24,16},{32,56},{40,32},{48,40},{56,48},{1,25}... | collective-permute-start | bytes 786440 | tf_op jit(solution)/shard_map/ppermute | solution.py:236
  16.3 3.9 %collective-permute-start.1 = (bf16[4,32,1024]{2,1,0:T(8,128)(2,1)}, bf16[4,32,1024]{2,1,0:T(8,128)(2,1)S(1)}, u32[]{:S(2)}, u32[]{:S(2)}) collective-permute-start(bf16[4,32,1024]{2,1,0:T(8,128)(2,1)} %get-tuple-element.15.refs_0_), channel_id=1, source_target_pairs={{0,8},{8,16},{16,24},{24,0},{32,40},{40,48},{48,56},{56,32},{1,9},... | collective-permute-start | bytes 786440 | tf_op jit(solution)/shard_map/ppermute | solution.py:236
  20.3 0.0 collective-permute-done.refs_1_
  20.3 1.9 %collective-permute-start.6 = (bf16[4,32,1024]{2,1,0:T(8,128)(2,1)S(1)}, bf16[4,32,1024]{2,1,0:T(8,128)(2,1)}, u32[]{:S(2)}, u32[]{:S(2)}) collective-permute-start(bf16[4,32,1024]{2,1,0:T(8,128)(2,1)S(1)} %collective-permute-done.refs_1_), channel_id=1, source_target_pairs={{0,16},{8,24},{16,0},{24,8},{32,48},{40,56},{48,32},{56,40},{1,17}... | collective-permute-start | bytes 786440 | tf_op jit(solution)/shard_map/ppermute | solution.py:236
  22.2 3.6 %collective-permute-start.5 = (bf16[4,32,1024]{2,1,0:T(8,128)(2,1)S(1)}, bf16[4,32,1024]{2,1,0:T(8,128)(2,1)}, u32[]{:S(2)}, u32[]{:S(2)}) collective-permute-start(bf16[4,32,1024]{2,1,0:T(8,128)(2,1)S(1)} %collective-permute-done.refs_1_), channel_id=1, source_target_pairs={{0,24},{8,0},{16,8},{24,16},{32,56},{40,32},{48,40},{56,48},{1,25}... | collective-permute-start | bytes 786440 | tf_op jit(solution)/shard_map/ppermute | solution.py:236
  25.9 0.0 collective-permute-done.3.refs_4_
  25.9 2.3 %collective-permute-start.4 = (bf16[4,32,1024]{2,1,0:T(8,128)(2,1)S(1)}, bf16[4,32,1024]{2,1,0:T(8,128)(2,1)}, u32[]{:S(2)}, u32[]{:S(2)}) collective-permute-start(bf16[4,32,1024]{2,1,0:T(8,128)(2,1)S(1)} %collective-permute-done.refs_1_), channel_id=1, source_target_pairs={{0,8},{8,16},{16,24},{24,0},{32,40},{40,48},{48,56},{56,32},{1,9},... | collective-permute-start | bytes 786440 | tf_op jit(solution)/shard_map/ppermute | solution.py:236
  28.1 0.0 copy-start
  28.1 0.0 copy-start.1
  28.2 14.1 %all-to-all-start = ((bf16[192,16,256]{2,1,0:T(8,128)(2,1)}), bf16[192,16,256]{2,1,0:T(8,128)(2,1)}, u32[]{:S(2)}, u32[]{:S(2)}) async-start(bf16[192,16,256]{2,1,0:T(8,128)(2,1)} %get-tuple-element.14), calls=%async_computation | async-start | bytes 3145728 | tf_op jit(solution)/shard_map/all_to_all | solution.py:329
  42.4 0.1 stack.53.place
  42.5 0.0 collective-permute-done.2.refs_3_
  42.5 0.0 collective-permute-done.1.refs_2_
  42.5 0.0 copy-start.2
  42.5 0.7 copy-done.2
  43.2 0.0 collective-permute-done.6.refs_7_
  43.2 0.0 collective-permute-done.5.refs_6_
  43.2 0.0 collective-permute-done.4.refs_5_
  43.2 0.0 copy-done
  43.2 0.0 copy-done.1
  43.2 0.0 copy-start.3
  43.2 0.9 %copy-done.3 = bf16[4,32,1024]{2,1,0:T(8,128)(2,1)S(1)} copy-done((bf16[4,32,1024]{2,1,0:T(8,128)(2,1)S(1)}, bf16[4,32,1024]{2,1,0:T(8,128)(2,1)}, u32[]{:S(2)}) %copy-start.3) | copy-done | bytes 262168
  44.2 3.5 %project.1 = (bf16[4,256,128]{2,1,0:T(8,128)(2,1)S(1)}, bf16[4,256,128]{2,1,0:T(8,128)(2,1)S(1)}, bf16[4,256,128]{2,1,0:T(8,128)(2,1)S(1)}, bf16[4,256,128]{2,1,...) custom-call(s32[1]{0:T(128)} %bitcast.1.me, ...), custom_call_target="tpu_custom_call" | custom-call | flops 21474836480 | bytes 6291456 | tf_op jit(solution)/shard_map/project/pallas_call | solution.py:216
  47.7 0.1 pad_maximum_fusion.1
  47.7 5.4 %collective-permute-start.8 = (bf16[2,4,256,128]{3,2,1,0:T(8,128)(2,1)S(1)}, bf16[2,4,256,128]{3,2,1,0:T(8,128)(2,1)S(1)}, u32[]{:S(2)}, u32[]{:S(2)}) collective-permute-start(bf16[2,4,256,128]{3,2,1,0:T(8,128)(2,1)S(1)} %pad_maximum_fusion.1), channel_id=1, source_target_pairs={{0,7},{1,0},{2,1},{3,2},{4,3},{5,4},{6,5},{7,6},{8,15},{9,8},{10,9... | collective-permute-start | bytes 1572872 | tf_op jit(solution)/shard_map/ppermute | solution.py:284
  53.2 1.9 %collective-permute-start.9 = (bf16[2,256,128]{2,1,0:T(8,128)(2,1)S(1)}, bf16[2,256,128]{2,1,0:T(8,128)(2,1)S(1)}, u32[]{:S(2)}, u32[]{:S(2)}) collective-permute-start(bf16[2,256,128]{2,1,0:T(8,128)(2,1)S(1)} %get-tuple-element.26), channel_id=1, source_target_pairs={{0,2},{1,3},{2,4},{3,5},{4,6},{5,7},{6,0},{7,1},{8,10},{9,11},{10,... | collective-permute-start | bytes 393224 | tf_op jit(solution)/shard_map/ppermute | solution.py:284
  55.1 6.0 %collective-permute-start.11 = (bf16[2,256,128]{2,1,0:T(8,128)(2,1)S(1)}, bf16[2,256,128]{2,1,0:T(8,128)(2,1)S(1)}, u32[]{:S(2)}, u32[]{:S(2)}) collective-permute-start(bf16[2,256,128]{2,1,0:T(8,128)(2,1)S(1)} %get-tuple-element.27), channel_id=1, source_target_pairs={{0,6},{1,7},{2,0},{3,1},{4,2},{5,3},{6,4},{7,5},{8,14},{9,15},{10,... | collective-permute-start | bytes 393224 | tf_op jit(solution)/shard_map/ppermute | solution.py:284
  61.1 0.1 pad_maximum_fusion
  61.2 1.9 %collective-permute-start.7 = (bf16[2,4,256,128]{3,2,1,0:T(8,128)(2,1)S(1)}, bf16[2,4,256,128]{3,2,1,0:T(8,128)(2,1)S(1)}, u32[]{:S(2)}, u32[]{:S(2)}) collective-permute-start(bf16[2,4,256,128]{3,2,1,0:T(8,128)(2,1)S(1)} %pad_maximum_fusion), channel_id=1, source_target_pairs={{0,1},{1,2},{2,3},{3,4},{4,5},{5,6},{6,7},{7,0},{8,9},{9,10},{10,1... | collective-permute-start | bytes 1572872 | tf_op jit(solution)/shard_map/ppermute | solution.py:284
  63.1 5.1 %collective-permute-done.8 = bf16[2,4,256,128]{3,2,1,0:T(8,128)(2,1)S(1)} collective-permute-done((bf16[2,4,256,128]{3,2,1,0:T(8,128)(2,1)S(1)}, bf16[2,4,256,128]{3,2,1,0:T(8,128)(2,1)S(1)}, u32[]{:S(2)}, u32[]{:S(2)}) %collective-permute-start.8) | collective-permute-done | bytes 524320 | tf_op jit(solution)/shard_map/ppermute | solution.py:284
  68.2 0.1 convert_add_fusion
  68.3 1.9 %collective-permute-done.11 = bf16[2,256,128]{2,1,0:T(8,128)(2,1)S(1)} collective-permute-done((bf16[2,256,128]{2,1,0:T(8,128)(2,1)S(1)}, bf16[2,256,128]{2,1,0:T(8,128)(2,1)S(1)}, u32[]{:S(2)}, u32[]{:S(2)}) %collective-permute-start.11) | collective-permute-done | bytes 131104 | tf_op jit(solution)/shard_map/ppermute | solution.py:284
  70.3 6.5 %collective-permute-start.12 = (bf16[4,256,128]{2,1,0:T(8,128)(2,1)S(1)}, bf16[4,256,128]{2,1,0:T(8,128)(2,1)S(1)}, u32[]{:S(2)}, u32[]{:S(2)}) collective-permute-start(bf16[4,256,128]{2,1,0:T(8,128)(2,1)S(1)} %pad_maximum_fusion.3), channel_id=1, source_target_pairs={{0,6},{1,7},{2,0},{3,1},{4,2},{5,3},{6,4},{7,5},{8,14},{9,15},{10,... | collective-permute-start | bytes 786440 | tf_op jit(solution)/shard_map/ppermute | solution.py:284
  76.8 0.6 collective-permute-done.7
  77.4 0.1 convert_add_fusion.1
  77.5 0.0 collective-permute-done.9
  77.6 1.9 %collective-permute-start.10 = (bf16[4,256,128]{2,1,0:T(8,128)(2,1)S(1)}, bf16[4,256,128]{2,1,0:T(8,128)(2,1)S(1)}, u32[]{:S(2)}, u32[]{:S(2)}) collective-permute-start(bf16[4,256,128]{2,1,0:T(8,128)(2,1)S(1)} %pad_maximum_fusion.2), channel_id=1, source_target_pairs={{0,2},{1,3},{2,4},{3,5},{4,6},{5,7},{6,0},{7,1},{8,10},{9,11},{10,... | collective-permute-start | bytes 786440 | tf_op jit(solution)/shard_map/ppermute | solution.py:284
  79.5 2.8 %all-to-all-done.source = bf16[192,16,256]{2,1,0:T(8,128)(2,1)} async-done(((bf16[192,16,256]{2,1,0:T(8,128)(2,1)}), bf16[192,16,256]{2,1,0:T(8,128)(2,1)}, u32[]{:S(2)}, u32[]{:S(2)}) %all-to-all-start) | async-done | bytes 1572896 | tf_op jit(solution)/shard_map/all_to_all | solution.py:329
  82.3 2.2 %move.1 = bf16[192,16,256]{2,1,0:T(8,128)(2,1)} custom-call(bf16[192,16,256]{2,1,0:T(8,128)(2,1)} %all-to-all-done.source), custom_call_target="tpu_custom_call" | custom-call | bytes 3145728 | tf_op jit(solution)/shard_map/move/pallas_call | solution.py:264
  84.5 1.8 %collective-permute-done.12 = bf16[4,256,128]{2,1,0:T(8,128)(2,1)S(1)} collective-permute-done((bf16[4,256,128]{2,1,0:T(8,128)(2,1)S(1)}, bf16[4,256,128]{2,1,0:T(8,128)(2,1)S(1)}, u32[]{:S(2)}, u32[]{:S(2)}) %collective-permute-start.12) | collective-permute-done | bytes 262176 | tf_op jit(solution)/shard_map/ppermute | solution.py:284
  86.3 6.7 %collective-permute-done.10 = bf16[4,256,128]{2,1,0:T(8,128)(2,1)S(1)} collective-permute-done((bf16[4,256,128]{2,1,0:T(8,128)(2,1)S(1)}, bf16[4,256,128]{2,1,0:T(8,128)(2,1)S(1)}, u32[]{:S(2)}, u32[]{:S(2)}) %collective-permute-start.10) | collective-permute-done | bytes 262176 | tf_op jit(solution)/shard_map/ppermute | solution.py:284
  92.9 0.9 fusion.2
  (7 shorter events, 0.2 us)
Async XLA Ops:
  4.7 15.6 %collective-permute-start = (bf16[4,32,1024]{2,1,0:T(8,128)(2,1)}, bf16[4,32,1024]{2,1,0:T(8,128)(2,1)S(1)}, u32[]{:S(2)}, u32[]{:S(2)}) collective-permute-start(bf16[4,32,1024]{2,1,0:T(8,128)(2,1)} %get-tuple-element.15.refs_0_), channel_id=1, source_target_pairs={{0,32},{8,40},{16,48},{24,56},{32,0},{40,8},{48,16},{56,24},{1,33}... | collective-permute-start | bytes 786440 | tf_op jit(solution)/shard_map/ppermute | solution.py:240
  9.0 16.9 %collective-permute-start.3 = (bf16[4,32,1024]{2,1,0:T(8,128)(2,1)}, bf16[4,32,1024]{2,1,0:T(8,128)(2,1)S(1)}, u32[]{:S(2)}, u32[]{:S(2)}) collective-permute-start(bf16[4,32,1024]{2,1,0:T(8,128)(2,1)} %get-tuple-element.15.refs_0_), channel_id=1, source_target_pairs={{0,16},{8,24},{16,0},{24,8},{32,48},{40,56},{48,32},{56,40},{1,17}... | collective-permute-start | bytes 786440 | tf_op jit(solution)/shard_map/ppermute | solution.py:236
  14.4 28.0 %collective-permute-start.2 = (bf16[4,32,1024]{2,1,0:T(8,128)(2,1)}, bf16[4,32,1024]{2,1,0:T(8,128)(2,1)S(1)}, u32[]{:S(2)}, u32[]{:S(2)}) collective-permute-start(bf16[4,32,1024]{2,1,0:T(8,128)(2,1)} %get-tuple-element.15.refs_0_), channel_id=1, source_target_pairs={{0,24},{8,0},{16,8},{24,16},{32,56},{40,32},{48,40},{56,48},{1,25}... | collective-permute-start | bytes 786440 | tf_op jit(solution)/shard_map/ppermute | solution.py:236
  16.3 26.1 %collective-permute-start.1 = (bf16[4,32,1024]{2,1,0:T(8,128)(2,1)}, bf16[4,32,1024]{2,1,0:T(8,128)(2,1)S(1)}, u32[]{:S(2)}, u32[]{:S(2)}) collective-permute-start(bf16[4,32,1024]{2,1,0:T(8,128)(2,1)} %get-tuple-element.15.refs_0_), channel_id=1, source_target_pairs={{0,8},{8,16},{16,24},{24,0},{32,40},{40,48},{48,56},{56,32},{1,9},... | collective-permute-start | bytes 786440 | tf_op jit(solution)/shard_map/ppermute | solution.py:236
  20.3 22.9 %collective-permute-start.6 = (bf16[4,32,1024]{2,1,0:T(8,128)(2,1)S(1)}, bf16[4,32,1024]{2,1,0:T(8,128)(2,1)}, u32[]{:S(2)}, u32[]{:S(2)}) collective-permute-start(bf16[4,32,1024]{2,1,0:T(8,128)(2,1)S(1)} %collective-permute-done.refs_1_), channel_id=1, source_target_pairs={{0,16},{8,24},{16,0},{24,8},{32,48},{40,56},{48,32},{56,40},{1,17}... | collective-permute-start | bytes 786440 | tf_op jit(solution)/shard_map/ppermute | solution.py:236
  22.2 21.0 %collective-permute-start.5 = (bf16[4,32,1024]{2,1,0:T(8,128)(2,1)S(1)}, bf16[4,32,1024]{2,1,0:T(8,128)(2,1)}, u32[]{:S(2)}, u32[]{:S(2)}) collective-permute-start(bf16[4,32,1024]{2,1,0:T(8,128)(2,1)S(1)} %collective-permute-done.refs_1_), channel_id=1, source_target_pairs={{0,24},{8,0},{16,8},{24,16},{32,56},{40,32},{48,40},{56,48},{1,25}... | collective-permute-start | bytes 786440 | tf_op jit(solution)/shard_map/ppermute | solution.py:236
  25.9 17.3 %collective-permute-start.4 = (bf16[4,32,1024]{2,1,0:T(8,128)(2,1)S(1)}, bf16[4,32,1024]{2,1,0:T(8,128)(2,1)}, u32[]{:S(2)}, u32[]{:S(2)}) collective-permute-start(bf16[4,32,1024]{2,1,0:T(8,128)(2,1)S(1)} %collective-permute-done.refs_1_), channel_id=1, source_target_pairs={{0,8},{8,16},{16,24},{24,0},{32,40},{40,48},{48,56},{56,32},{1,9},... | collective-permute-start | bytes 786440 | tf_op jit(solution)/shard_map/ppermute | solution.py:236
  28.1 15.1 %copy-start = (bf16[1024,1024]{1,0:T(8,128)(2,1)S(1)}, bf16[1024,1024]{1,0:T(8,128)(2,1)}, u32[]{:S(2)}) copy-start(bf16[1024,1024]{1,0:T(8,128)(2,1)} %refs_8_.1) | copy-start | bytes 6291460
  28.1 15.0 %copy-start.1 = (bf16[4,32,1024]{2,1,0:T(8,128)(2,1)S(1)}, bf16[4,32,1024]{2,1,0:T(8,128)(2,1)}, u32[]{:S(2)}) copy-start(bf16[4,32,1024]{2,1,0:T(8,128)(2,1)} %get-tuple-element.15.refs_0_) | copy-start | bytes 786436
  28.2 54.1 %all-to-all-start = ((bf16[192,16,256]{2,1,0:T(8,128)(2,1)}), bf16[192,16,256]{2,1,0:T(8,128)(2,1)}, u32[]{:S(2)}, u32[]{:S(2)}) async-start(bf16[192,16,256]{2,1,0:T(8,128)(2,1)} %get-tuple-element.14), calls=%async_computation | async-start | bytes 3145728 | tf_op jit(solution)/shard_map/all_to_all | solution.py:329
  42.5 0.7 copy-start.2
  43.2 1.0 %copy-start.3 = (bf16[4,32,1024]{2,1,0:T(8,128)(2,1)S(1)}, bf16[4,32,1024]{2,1,0:T(8,128)(2,1)}, u32[]{:S(2)}) copy-start(bf16[4,32,1024]{2,1,0:T(8,128)(2,1)} %copy-done.2) | copy-start | bytes 786436
  47.7 20.5 %collective-permute-start.8 = (bf16[2,4,256,128]{3,2,1,0:T(8,128)(2,1)S(1)}, bf16[2,4,256,128]{3,2,1,0:T(8,128)(2,1)S(1)}, u32[]{:S(2)}, u32[]{:S(2)}) collective-permute-start(bf16[2,4,256,128]{3,2,1,0:T(8,128)(2,1)S(1)} %pad_maximum_fusion.1), channel_id=1, source_target_pairs={{0,7},{1,0},{2,1},{3,2},{4,3},{5,4},{6,5},{7,6},{8,15},{9,8},{10,9... | collective-permute-start | bytes 1572872 | tf_op jit(solution)/shard_map/ppermute | solution.py:284
  53.2 24.4 %collective-permute-start.9 = (bf16[2,256,128]{2,1,0:T(8,128)(2,1)S(1)}, bf16[2,256,128]{2,1,0:T(8,128)(2,1)S(1)}, u32[]{:S(2)}, u32[]{:S(2)}) collective-permute-start(bf16[2,256,128]{2,1,0:T(8,128)(2,1)S(1)} %get-tuple-element.26), channel_id=1, source_target_pairs={{0,2},{1,3},{2,4},{3,5},{4,6},{5,7},{6,0},{7,1},{8,10},{9,11},{10,... | collective-permute-start | bytes 393224 | tf_op jit(solution)/shard_map/ppermute | solution.py:284
  55.1 15.2 %collective-permute-start.11 = (bf16[2,256,128]{2,1,0:T(8,128)(2,1)S(1)}, bf16[2,256,128]{2,1,0:T(8,128)(2,1)S(1)}, u32[]{:S(2)}, u32[]{:S(2)}) collective-permute-start(bf16[2,256,128]{2,1,0:T(8,128)(2,1)S(1)} %get-tuple-element.27), channel_id=1, source_target_pairs={{0,6},{1,7},{2,0},{3,1},{4,2},{5,3},{6,4},{7,5},{8,14},{9,15},{10,... | collective-permute-start | bytes 393224 | tf_op jit(solution)/shard_map/ppermute | solution.py:284
  61.2 16.2 %collective-permute-start.7 = (bf16[2,4,256,128]{3,2,1,0:T(8,128)(2,1)S(1)}, bf16[2,4,256,128]{3,2,1,0:T(8,128)(2,1)S(1)}, u32[]{:S(2)}, u32[]{:S(2)}) collective-permute-start(bf16[2,4,256,128]{3,2,1,0:T(8,128)(2,1)S(1)} %pad_maximum_fusion), channel_id=1, source_target_pairs={{0,1},{1,2},{2,3},{3,4},{4,5},{5,6},{6,7},{7,0},{8,9},{9,10},{10,1... | collective-permute-start | bytes 1572872 | tf_op jit(solution)/shard_map/ppermute | solution.py:284
  70.3 16.0 %collective-permute-start.12 = (bf16[4,256,128]{2,1,0:T(8,128)(2,1)S(1)}, bf16[4,256,128]{2,1,0:T(8,128)(2,1)S(1)}, u32[]{:S(2)}, u32[]{:S(2)}) collective-permute-start(bf16[4,256,128]{2,1,0:T(8,128)(2,1)S(1)} %pad_maximum_fusion.3), channel_id=1, source_target_pairs={{0,6},{1,7},{2,0},{3,1},{4,2},{5,3},{6,4},{7,5},{8,14},{9,15},{10,... | collective-permute-start | bytes 786440 | tf_op jit(solution)/shard_map/ppermute | solution.py:284
  77.6 15.3 %collective-permute-start.10 = (bf16[4,256,128]{2,1,0:T(8,128)(2,1)S(1)}, bf16[4,256,128]{2,1,0:T(8,128)(2,1)S(1)}, u32[]{:S(2)}, u32[]{:S(2)}) collective-permute-start(bf16[4,256,128]{2,1,0:T(8,128)(2,1)S(1)} %pad_maximum_fusion.2), channel_id=1, source_target_pairs={{0,2},{1,3},{2,4},{3,5},{4,6},{5,7},{6,0},{7,1},{8,10},{9,11},{10,... | collective-permute-start | bytes 786440 | tf_op jit(solution)/shard_map/ppermute | solution.py:284

commit v5 on v4

--- a/solution.py
+++ b/solution.py
@@ -240,7 +240,7 @@
     other = lax.ppermute(heads, "seq", [(i, (i + along) % (2 * along)) for i in range(2 * along)])
     parts, place = [heads, other], [me, (1 - z) * along + x]
     for row, block in ((z, heads), (1 - z, other)):
-        for by in (1, -1, 2):
+        for by in ((2, -1, 1) if block is heads else (1, -1, 2)):
             parts.append(shift(block, by))
             place.append(row * along + (x - by) % along)
     return parts, jnp.stack(place)

time: 94.5 us -> 94.4 us (level)
    all_to_all x1, starting transfers between devices: 14.1 us -> 13 us  [per_device(): lax.all_to_all(packed, ('grp', 'seq'), split_axis=0, concat_axis=0, tiled...]
    ppermute x6, starting transfers between devices: 19.1 us -> 20.2 us  [shift(): return lax.ppermute(block, 'seq', pairs)]
where the time goes in v5:
time: 94.4 us; the launch traced here: 93.8 us
  starting transfers between devices  61.2 us (65%)
  waiting for transfers between devices  18.9 us (20%)
  Pallas kernels  9.76 us (10%)
  local copies, waits for them, and re-layouts  1.8 us (2%)
  other arithmetic  1.2 us (1%)
  between operations  1 us (1%)
    ppermute x6, starting transfers between devices, shift(): lax.ppermute(block, 'tp', [(i, (i + by) % size) for i in range(size)])  23.7 us
    ppermute x6, starting transfers between devices, shift(): return lax.ppermute(block, 'seq', pairs)  20.2 us
    ppermute x6, waiting for transfers between devices, shift(): lax.ppermute(block, 'tp', [(i, (i + by) % size) for i in range(size)])  16.1 us
    all_to_all x1, starting transfers between devices, per_device(): lax.all_to_all(packed, ('grp', 'seq'), split_axis=0, concat_axis=0, tiled...  13 us
    ppermute x1, starting transfers between devices, gather_heads(): lax.ppermute(heads, 'seq', [(i, (i + along) % (2 * along)) for i in range...  4.28 us
    pallas_call x1, Pallas kernels, attend_and_pack(): pl.pallas_call(attend_kernel, out_shape=[jax.ShapeDtypeStruct(queries.sha...  4.05 us
    pallas_call x1, Pallas kernels, project(): pl.pallas_call(project_kernel, out_shape=[block] * len(OFFSETS), in_specs...  3.52 us
    all_to_all x1, waiting for transfers between devices, per_device(): lax.all_to_all(packed, ('grp', 'seq'), split_axis=0, concat_axis=0, tiled...  2.75 us
  transfers between devices with their start and end apart: 14, of which 6 were waited for; matrix products, arithmetic and copies ran while one was open for 0% of the time, Pallas kernels for 6%

profile of v5, /device:TPU:4, one launch (start us, length us, event | category | flops | bytes accessed | tf_op | source)
XLA Modules:
  0.0 93.8 jit_solution(3432102753632430221)
XLA Ops:
  0.6 4.0 %attend_and_pack.1 = (bf16[4,32,1024]{2,1,0:T(8,128)(2,1)}, bf16[192,16,256]{2,1,0:T(8,128)(2,1)}) custom-call(s32[1,32]{1,0:T(1,128)} %blocks_hbm.1, s32[1,32]{1,0:T(1,128)} %tail_hbm.1, s32[1,32]{1,0:T(1,128)} %owner_hbm.1, bf16[64,16,256]{2,1,0:T(8,128)(2,1)} %finished_hbm.1, s32[2,32]{1,0:T(2,128)} %bitcast.38, s32[1,32]{1,0:T(1,128)} %length_hbm.1, ...), custom_call_target="tpu_custom_call" | custom-call | flops 301989888 | bytes 5242880 | tf_op jit(solution)/shard_map/attend_and_pack/pallas_call | solution.py:155
  4.7 4.3 %collective-permute-start = (bf16[4,32,1024]{2,1,0:T(8,128)(2,1)}, bf16[4,32,1024]{2,1,0:T(8,128)(2,1)S(1)}, u32[]{:S(2)}, u32[]{:S(2)}) collective-permute-start(bf16[4,32,1024]{2,1,0:T(8,128)(2,1)} %get-tuple-element.15.refs_0_), channel_id=1, source_target_pairs={{0,32},{8,40},{16,48},{24,56},{32,0},{40,8},{48,16},{56,24},{1,33}... | collective-permute-start | bytes 786440 | tf_op jit(solution)/shard_map/ppermute | solution.py:240
  9.0 3.1 %collective-permute-start.3 = (bf16[4,32,1024]{2,1,0:T(8,128)(2,1)}, bf16[4,32,1024]{2,1,0:T(8,128)(2,1)S(1)}, u32[]{:S(2)}, u32[]{:S(2)}) collective-permute-start(bf16[4,32,1024]{2,1,0:T(8,128)(2,1)} %get-tuple-element.15.refs_0_), channel_id=1, source_target_pairs={{0,8},{8,16},{16,24},{24,0},{32,40},{40,48},{48,56},{56,32},{1,9},... | collective-permute-start | bytes 786440 | tf_op jit(solution)/shard_map/ppermute | solution.py:236
  12.1 2.7 %collective-permute-start.2 = (bf16[4,32,1024]{2,1,0:T(8,128)(2,1)}, bf16[4,32,1024]{2,1,0:T(8,128)(2,1)S(1)}, u32[]{:S(2)}, u32[]{:S(2)}) collective-permute-start(bf16[4,32,1024]{2,1,0:T(8,128)(2,1)} %get-tuple-element.15.refs_0_), channel_id=1, source_target_pairs={{0,24},{8,0},{16,8},{24,16},{32,56},{40,32},{48,40},{56,48},{1,25}... | collective-permute-start | bytes 786440 | tf_op jit(solution)/shard_map/ppermute | solution.py:236
  14.8 6.6 %collective-permute-start.1 = (bf16[4,32,1024]{2,1,0:T(8,128)(2,1)}, bf16[4,32,1024]{2,1,0:T(8,128)(2,1)S(1)}, u32[]{:S(2)}, u32[]{:S(2)}) collective-permute-start(bf16[4,32,1024]{2,1,0:T(8,128)(2,1)} %get-tuple-element.15.refs_0_), channel_id=1, source_target_pairs={{0,16},{8,24},{16,0},{24,8},{32,48},{40,56},{48,32},{56,40},{1,17}... | collective-permute-start | bytes 786440 | tf_op jit(solution)/shard_map/ppermute | solution.py:236
  21.5 0.0 collective-permute-done.refs_1_
  21.5 1.9 %collective-permute-start.6 = (bf16[4,32,1024]{2,1,0:T(8,128)(2,1)S(1)}, bf16[4,32,1024]{2,1,0:T(8,128)(2,1)}, u32[]{:S(2)}, u32[]{:S(2)}) collective-permute-start(bf16[4,32,1024]{2,1,0:T(8,128)(2,1)S(1)} %collective-permute-done.refs_1_), channel_id=1, source_target_pairs={{0,16},{8,24},{16,0},{24,8},{32,48},{40,56},{48,32},{56,40},{1,17}... | collective-permute-start | bytes 786440 | tf_op jit(solution)/shard_map/ppermute | solution.py:236
  23.4 2.8 %collective-permute-start.5 = (bf16[4,32,1024]{2,1,0:T(8,128)(2,1)S(1)}, bf16[4,32,1024]{2,1,0:T(8,128)(2,1)}, u32[]{:S(2)}, u32[]{:S(2)}) collective-permute-start(bf16[4,32,1024]{2,1,0:T(8,128)(2,1)S(1)} %collective-permute-done.refs_1_), channel_id=1, source_target_pairs={{0,24},{8,0},{16,8},{24,16},{32,56},{40,32},{48,40},{56,48},{1,25}... | collective-permute-start | bytes 786440 | tf_op jit(solution)/shard_map/ppermute | solution.py:236
  26.2 0.0 collective-permute-done.3.refs_4_
  26.2 3.1 %collective-permute-start.4 = (bf16[4,32,1024]{2,1,0:T(8,128)(2,1)S(1)}, bf16[4,32,1024]{2,1,0:T(8,128)(2,1)}, u32[]{:S(2)}, u32[]{:S(2)}) collective-permute-start(bf16[4,32,1024]{2,1,0:T(8,128)(2,1)S(1)} %collective-permute-done.refs_1_), channel_id=1, source_target_pairs={{0,8},{8,16},{16,24},{24,0},{32,40},{40,48},{48,56},{56,32},{1,9},... | collective-permute-start | bytes 786440 | tf_op jit(solution)/shard_map/ppermute | solution.py:236
  29.3 0.0 copy-start
  29.3 0.0 copy-start.1
  29.3 13.0 %all-to-all-start = ((bf16[192,16,256]{2,1,0:T(8,128)(2,1)}), bf16[192,16,256]{2,1,0:T(8,128)(2,1)}, u32[]{:S(2)}, u32[]{:S(2)}) async-start(bf16[192,16,256]{2,1,0:T(8,128)(2,1)} %get-tuple-element.14), calls=%async_computation | async-start | bytes 3145728 | tf_op jit(solution)/shard_map/all_to_all | solution.py:329
  42.4 0.1 stack.53.place
  42.5 0.0 collective-permute-done.2.refs_3_
  42.5 0.0 collective-permute-done.1.refs_2_
  42.5 0.0 copy-start.2
  42.5 0.7 copy-done.2
  43.2 0.0 collective-permute-done.6.refs_7_
  43.2 0.0 collective-permute-done.5.refs_6_
  43.2 0.0 collective-permute-done.4.refs_5_
  43.2 0.0 copy-done
  43.2 0.0 copy-done.1
  43.2 0.0 copy-start.3
  43.2 0.9 %copy-done.3 = bf16[4,32,1024]{2,1,0:T(8,128)(2,1)S(1)} copy-done((bf16[4,32,1024]{2,1,0:T(8,128)(2,1)S(1)}, bf16[4,32,1024]{2,1,0:T(8,128)(2,1)}, u32[]{:S(2)}) %copy-start.3) | copy-done | bytes 262168
  44.2 3.5 %project.1 = (bf16[4,256,128]{2,1,0:T(8,128)(2,1)S(1)}, bf16[4,256,128]{2,1,0:T(8,128)(2,1)S(1)}, bf16[4,256,128]{2,1,0:T(8,128)(2,1)S(1)}, bf16[4,256,128]{2,1,...) custom-call(s32[1]{0:T(128)} %bitcast.1.me, ...), custom_call_target="tpu_custom_call" | custom-call | flops 21474836480 | bytes 6291456 | tf_op jit(solution)/shard_map/project/pallas_call | solution.py:216
  47.7 0.1 pad_maximum_fusion.1
  47.7 5.4 %collective-permute-start.8 = (bf16[2,4,256,128]{3,2,1,0:T(8,128)(2,1)S(1)}, bf16[2,4,256,128]{3,2,1,0:T(8,128)(2,1)S(1)}, u32[]{:S(2)}, u32[]{:S(2)}) collective-permute-start(bf16[2,4,256,128]{3,2,1,0:T(8,128)(2,1)S(1)} %pad_maximum_fusion.1), channel_id=1, source_target_pairs={{0,7},{1,0},{2,1},{3,2},{4,3},{5,4},{6,5},{7,6},{8,15},{9,8},{10,9... | collective-permute-start | bytes 1572872 | tf_op jit(solution)/shard_map/ppermute | solution.py:284
  53.2 1.9 %collective-permute-start.9 = (bf16[2,256,128]{2,1,0:T(8,128)(2,1)S(1)}, bf16[2,256,128]{2,1,0:T(8,128)(2,1)S(1)}, u32[]{:S(2)}, u32[]{:S(2)}) collective-permute-start(bf16[2,256,128]{2,1,0:T(8,128)(2,1)S(1)} %get-tuple-element.26), channel_id=1, source_target_pairs={{0,2},{1,3},{2,4},{3,5},{4,6},{5,7},{6,0},{7,1},{8,10},{9,11},{10,... | collective-permute-start | bytes 393224 | tf_op jit(solution)/shard_map/ppermute | solution.py:284
  55.1 6.0 %collective-permute-start.11 = (bf16[2,256,128]{2,1,0:T(8,128)(2,1)S(1)}, bf16[2,256,128]{2,1,0:T(8,128)(2,1)S(1)}, u32[]{:S(2)}, u32[]{:S(2)}) collective-permute-start(bf16[2,256,128]{2,1,0:T(8,128)(2,1)S(1)} %get-tuple-element.27), channel_id=1, source_target_pairs={{0,6},{1,7},{2,0},{3,1},{4,2},{5,3},{6,4},{7,5},{8,14},{9,15},{10,... | collective-permute-start | bytes 393224 | tf_op jit(solution)/shard_map/ppermute | solution.py:284
  61.1 0.1 pad_maximum_fusion
  61.2 1.9 %collective-permute-start.7 = (bf16[2,4,256,128]{3,2,1,0:T(8,128)(2,1)S(1)}, bf16[2,4,256,128]{3,2,1,0:T(8,128)(2,1)S(1)}, u32[]{:S(2)}, u32[]{:S(2)}) collective-permute-start(bf16[2,4,256,128]{3,2,1,0:T(8,128)(2,1)S(1)} %pad_maximum_fusion), channel_id=1, source_target_pairs={{0,1},{1,2},{2,3},{3,4},{4,5},{5,6},{6,7},{7,0},{8,9},{9,10},{10,1... | collective-permute-start | bytes 1572872 | tf_op jit(solution)/shard_map/ppermute | solution.py:284
  63.1 5.1 %collective-permute-done.8 = bf16[2,4,256,128]{3,2,1,0:T(8,128)(2,1)S(1)} collective-permute-done((bf16[2,4,256,128]{3,2,1,0:T(8,128)(2,1)S(1)}, bf16[2,4,256,128]{3,2,1,0:T(8,128)(2,1)S(1)}, u32[]{:S(2)}, u32[]{:S(2)}) %collective-permute-start.8) | collective-permute-done | bytes 524320 | tf_op jit(solution)/shard_map/ppermute | solution.py:284
  68.2 0.1 convert_add_fusion
  68.3 1.9 %collective-permute-done.11 = bf16[2,256,128]{2,1,0:T(8,128)(2,1)S(1)} collective-permute-done((bf16[2,256,128]{2,1,0:T(8,128)(2,1)S(1)}, bf16[2,256,128]{2,1,0:T(8,128)(2,1)S(1)}, u32[]{:S(2)}, u32[]{:S(2)}) %collective-permute-start.11) | collective-permute-done | bytes 131104 | tf_op jit(solution)/shard_map/ppermute | solution.py:284
  70.3 6.5 %collective-permute-start.12 = (bf16[4,256,128]{2,1,0:T(8,128)(2,1)S(1)}, bf16[4,256,128]{2,1,0:T(8,128)(2,1)S(1)}, u32[]{:S(2)}, u32[]{:S(2)}) collective-permute-start(bf16[4,256,128]{2,1,0:T(8,128)(2,1)S(1)} %pad_maximum_fusion.3), channel_id=1, source_target_pairs={{0,6},{1,7},{2,0},{3,1},{4,2},{5,3},{6,4},{7,5},{8,14},{9,15},{10,... | collective-permute-start | bytes 786440 | tf_op jit(solution)/shard_map/ppermute | solution.py:284
  76.8 0.6 collective-permute-done.7
  77.4 0.1 convert_add_fusion.1
  77.5 0.0 collective-permute-done.9
  77.6 1.9 %collective-permute-start.10 = (bf16[4,256,128]{2,1,0:T(8,128)(2,1)S(1)}, bf16[4,256,128]{2,1,0:T(8,128)(2,1)S(1)}, u32[]{:S(2)}, u32[]{:S(2)}) collective-permute-start(bf16[4,256,128]{2,1,0:T(8,128)(2,1)S(1)} %pad_maximum_fusion.2), channel_id=1, source_target_pairs={{0,2},{1,3},{2,4},{3,5},{4,6},{5,7},{6,0},{7,1},{8,10},{9,11},{10,... | collective-permute-start | bytes 786440 | tf_op jit(solution)/shard_map/ppermute | solution.py:284
  79.5 2.7 %all-to-all-done.source = bf16[192,16,256]{2,1,0:T(8,128)(2,1)} async-done(((bf16[192,16,256]{2,1,0:T(8,128)(2,1)}), bf16[192,16,256]{2,1,0:T(8,128)(2,1)}, u32[]{:S(2)}, u32[]{:S(2)}) %all-to-all-start) | async-done | bytes 1572896 | tf_op jit(solution)/shard_map/all_to_all | solution.py:329
  82.3 2.2 %move.1 = bf16[192,16,256]{2,1,0:T(8,128)(2,1)} custom-call(bf16[192,16,256]{2,1,0:T(8,128)(2,1)} %all-to-all-done.source), custom_call_target="tpu_custom_call" | custom-call | bytes 3145728 | tf_op jit(solution)/shard_map/move/pallas_call | solution.py:264
  84.5 1.8 %collective-permute-done.12 = bf16[4,256,128]{2,1,0:T(8,128)(2,1)S(1)} collective-permute-done((bf16[4,256,128]{2,1,0:T(8,128)(2,1)S(1)}, bf16[4,256,128]{2,1,0:T(8,128)(2,1)S(1)}, u32[]{:S(2)}, u32[]{:S(2)}) %collective-permute-start.12) | collective-permute-done | bytes 262176 | tf_op jit(solution)/shard_map/ppermute | solution.py:284
  86.3 6.6 %collective-permute-done.10 = bf16[4,256,128]{2,1,0:T(8,128)(2,1)S(1)} collective-permute-done((bf16[4,256,128]{2,1,0:T(8,128)(2,1)S(1)}, bf16[4,256,128]{2,1,0:T(8,128)(2,1)S(1)}, u32[]{:S(2)}, u32[]{:S(2)}) %collective-permute-start.10) | collective-permute-done | bytes 262176 | tf_op jit(solution)/shard_map/ppermute | solution.py:284
  92.9 0.9 fusion.2
  (7 shorter events, 0.2 us)
Async XLA Ops:
  4.7 16.8 %collective-permute-start = (bf16[4,32,1024]{2,1,0:T(8,128)(2,1)}, bf16[4,32,1024]{2,1,0:T(8,128)(2,1)S(1)}, u32[]{:S(2)}, u32[]{:S(2)}) collective-permute-start(bf16[4,32,1024]{2,1,0:T(8,128)(2,1)} %get-tuple-element.15.refs_0_), channel_id=1, source_target_pairs={{0,32},{8,40},{16,48},{24,56},{32,0},{40,8},{48,16},{56,24},{1,33}... | collective-permute-start | bytes 786440 | tf_op jit(solution)/shard_map/ppermute | solution.py:240
  9.0 17.2 %collective-permute-start.3 = (bf16[4,32,1024]{2,1,0:T(8,128)(2,1)}, bf16[4,32,1024]{2,1,0:T(8,128)(2,1)S(1)}, u32[]{:S(2)}, u32[]{:S(2)}) collective-permute-start(bf16[4,32,1024]{2,1,0:T(8,128)(2,1)} %get-tuple-element.15.refs_0_), channel_id=1, source_target_pairs={{0,8},{8,16},{16,24},{24,0},{32,40},{40,48},{48,56},{56,32},{1,9},... | collective-permute-start | bytes 786440 | tf_op jit(solution)/shard_map/ppermute | solution.py:236
  12.1 30.4 %collective-permute-start.2 = (bf16[4,32,1024]{2,1,0:T(8,128)(2,1)}, bf16[4,32,1024]{2,1,0:T(8,128)(2,1)S(1)}, u32[]{:S(2)}, u32[]{:S(2)}) collective-permute-start(bf16[4,32,1024]{2,1,0:T(8,128)(2,1)} %get-tuple-element.15.refs_0_), channel_id=1, source_target_pairs={{0,24},{8,0},{16,8},{24,16},{32,56},{40,32},{48,40},{56,48},{1,25}... | collective-permute-start | bytes 786440 | tf_op jit(solution)/shard_map/ppermute | solution.py:236
  14.8 27.6 %collective-permute-start.1 = (bf16[4,32,1024]{2,1,0:T(8,128)(2,1)}, bf16[4,32,1024]{2,1,0:T(8,128)(2,1)S(1)}, u32[]{:S(2)}, u32[]{:S(2)}) collective-permute-start(bf16[4,32,1024]{2,1,0:T(8,128)(2,1)} %get-tuple-element.15.refs_0_), channel_id=1, source_target_pairs={{0,16},{8,24},{16,0},{24,8},{32,48},{40,56},{48,32},{56,40},{1,17}... | collective-permute-start | bytes 786440 | tf_op jit(solution)/shard_map/ppermute | solution.py:236
  21.5 21.7 %collective-permute-start.6 = (bf16[4,32,1024]{2,1,0:T(8,128)(2,1)S(1)}, bf16[4,32,1024]{2,1,0:T(8,128)(2,1)}, u32[]{:S(2)}, u32[]{:S(2)}) collective-permute-start(bf16[4,32,1024]{2,1,0:T(8,128)(2,1)S(1)} %collective-permute-done.refs_1_), channel_id=1, source_target_pairs={{0,16},{8,24},{16,0},{24,8},{32,48},{40,56},{48,32},{56,40},{1,17}... | collective-permute-start | bytes 786440 | tf_op jit(solution)/shard_map/ppermute | solution.py:236
  23.4 19.8 %collective-permute-start.5 = (bf16[4,32,1024]{2,1,0:T(8,128)(2,1)S(1)}, bf16[4,32,1024]{2,1,0:T(8,128)(2,1)}, u32[]{:S(2)}, u32[]{:S(2)}) collective-permute-start(bf16[4,32,1024]{2,1,0:T(8,128)(2,1)S(1)} %collective-permute-done.refs_1_), channel_id=1, source_target_pairs={{0,24},{8,0},{16,8},{24,16},{32,56},{40,32},{48,40},{56,48},{1,25}... | collective-permute-start | bytes 786440 | tf_op jit(solution)/shard_map/ppermute | solution.py:236
  26.2 17.0 %collective-permute-start.4 = (bf16[4,32,1024]{2,1,0:T(8,128)(2,1)S(1)}, bf16[4,32,1024]{2,1,0:T(8,128)(2,1)}, u32[]{:S(2)}, u32[]{:S(2)}) collective-permute-start(bf16[4,32,1024]{2,1,0:T(8,128)(2,1)S(1)} %collective-permute-done.refs_1_), channel_id=1, source_target_pairs={{0,8},{8,16},{16,24},{24,0},{32,40},{40,48},{48,56},{56,32},{1,9},... | collective-permute-start | bytes 786440 | tf_op jit(solution)/shard_map/ppermute | solution.py:236
  29.3 13.9 %copy-start = (bf16[1024,1024]{1,0:T(8,128)(2,1)S(1)}, bf16[1024,1024]{1,0:T(8,128)(2,1)}, u32[]{:S(2)}) copy-start(bf16[1024,1024]{1,0:T(8,128)(2,1)} %refs_8_.1) | copy-start | bytes 6291460
  29.3 13.9 %copy-start.1 = (bf16[4,32,1024]{2,1,0:T(8,128)(2,1)S(1)}, bf16[4,32,1024]{2,1,0:T(8,128)(2,1)}, u32[]{:S(2)}) copy-start(bf16[4,32,1024]{2,1,0:T(8,128)(2,1)} %get-tuple-element.15.refs_0_) | copy-start | bytes 786436
  29.3 53.0 %all-to-all-start = ((bf16[192,16,256]{2,1,0:T(8,128)(2,1)}), bf16[192,16,256]{2,1,0:T(8,128)(2,1)}, u32[]{:S(2)}, u32[]{:S(2)}) async-start(bf16[192,16,256]{2,1,0:T(8,128)(2,1)} %get-tuple-element.14), calls=%async_computation | async-start | bytes 3145728 | tf_op jit(solution)/shard_map/all_to_all | solution.py:329
  42.5 0.7 copy-start.2
  43.2 1.0 %copy-start.3 = (bf16[4,32,1024]{2,1,0:T(8,128)(2,1)S(1)}, bf16[4,32,1024]{2,1,0:T(8,128)(2,1)}, u32[]{:S(2)}) copy-start(bf16[4,32,1024]{2,1,0:T(8,128)(2,1)} %copy-done.2) | copy-start | bytes 786436
  47.7 20.5 %collective-permute-start.8 = (bf16[2,4,256,128]{3,2,1,0:T(8,128)(2,1)S(1)}, bf16[2,4,256,128]{3,2,1,0:T(8,128)(2,1)S(1)}, u32[]{:S(2)}, u32[]{:S(2)}) collective-permute-start(bf16[2,4,256,128]{3,2,1,0:T(8,128)(2,1)S(1)} %pad_maximum_fusion.1), channel_id=1, source_target_pairs={{0,7},{1,0},{2,1},{3,2},{4,3},{5,4},{6,5},{7,6},{8,15},{9,8},{10,9... | collective-permute-start | bytes 1572872 | tf_op jit(solution)/shard_map/ppermute | solution.py:284
  53.2 24.4 %collective-permute-start.9 = (bf16[2,256,128]{2,1,0:T(8,128)(2,1)S(1)}, bf16[2,256,128]{2,1,0:T(8,128)(2,1)S(1)}, u32[]{:S(2)}, u32[]{:S(2)}) collective-permute-start(bf16[2,256,128]{2,1,0:T(8,128)(2,1)S(1)} %get-tuple-element.26), channel_id=1, source_target_pairs={{0,2},{1,3},{2,4},{3,5},{4,6},{5,7},{6,0},{7,1},{8,10},{9,11},{10,... | collective-permute-start | bytes 393224 | tf_op jit(solution)/shard_map/ppermute | solution.py:284
  55.1 15.2 %collective-permute-start.11 = (bf16[2,256,128]{2,1,0:T(8,128)(2,1)S(1)}, bf16[2,256,128]{2,1,0:T(8,128)(2,1)S(1)}, u32[]{:S(2)}, u32[]{:S(2)}) collective-permute-start(bf16[2,256,128]{2,1,0:T(8,128)(2,1)S(1)} %get-tuple-element.27), channel_id=1, source_target_pairs={{0,6},{1,7},{2,0},{3,1},{4,2},{5,3},{6,4},{7,5},{8,14},{9,15},{10,... | collective-permute-start | bytes 393224 | tf_op jit(solution)/shard_map/ppermute | solution.py:284
  61.2 16.2 %collective-permute-start.7 = (bf16[2,4,256,128]{3,2,1,0:T(8,128)(2,1)S(1)}, bf16[2,4,256,128]{3,2,1,0:T(8,128)(2,1)S(1)}, u32[]{:S(2)}, u32[]{:S(2)}) collective-permute-start(bf16[2,4,256,128]{3,2,1,0:T(8,128)(2,1)S(1)} %pad_maximum_fusion), channel_id=1, source_target_pairs={{0,1},{1,2},{2,3},{3,4},{4,5},{5,6},{6,7},{7,0},{8,9},{9,10},{10,1... | collective-permute-start | bytes 1572872 | tf_op jit(solution)/shard_map/ppermute | solution.py:284
  70.3 16.0 %collective-permute-start.12 = (bf16[4,256,128]{2,1,0:T(8,128)(2,1)S(1)}, bf16[4,256,128]{2,1,0:T(8,128)(2,1)S(1)}, u32[]{:S(2)}, u32[]{:S(2)}) collective-permute-start(bf16[4,256,128]{2,1,0:T(8,128)(2,1)S(1)} %pad_maximum_fusion.3), channel_id=1, source_target_pairs={{0,6},{1,7},{2,0},{3,1},{4,2},{5,3},{6,4},{7,5},{8,14},{9,15},{10,... | collective-permute-start | bytes 786440 | tf_op jit(solution)/shard_map/ppermute | solution.py:284
  77.6 15.3 %collective-permute-start.10 = (bf16[4,256,128]{2,1,0:T(8,128)(2,1)S(1)}, bf16[4,256,128]{2,1,0:T(8,128)(2,1)S(1)}, u32[]{:S(2)}, u32[]{:S(2)}) collective-permute-start(bf16[4,256,128]{2,1,0:T(8,128)(2,1)S(1)} %pad_maximum_fusion.2), channel_id=1, source_target_pairs={{0,2},{1,3},{2,4},{3,5},{4,6},{5,7},{6,0},{7,1},{8,10},{9,11},{10,... | collective-permute-start | bytes 786440 | tf_op jit(solution)/shard_map/ppermute | solution.py:284
